TPU v7x, 256 devices: a whole 4x4x8 slice. The times are simulated.
256 devices in a mesh: dp: 8 (over x, core), ts: 32 (over z, y).
Axes of the slice: x: 4, y: 4, z: 8, core: 2. Of those that a mesh axis runs over, the one named last changes fastest.
Arguments:
- block_activity: bfloat16 [8, 2048, 3584], P('dp', 'ts'), may hold values from -6 to 6
- result_cotangent: bfloat16 [8, 2048, 3584], P('dp', 'ts'), may hold values from -6 to 6
- kept_locations: int32 [8, 256], P('dp'), may hold values from 0 to 2047, as said below
- prenormal_scaling: bfloat16 [3584], replicated, may hold values from 0.5 to 1.5
- scorer_matrix: bfloat16 [3584], replicated, may hold values from -0.09375 to 0.09375
- switch_matrix: bfloat16 [3584, 14336], P(None, 'ts'), may hold values from -0.09375 to 0.09375
- expand_matrix: bfloat16 [3584, 14336], P(None, 'ts'), may hold values from -0.09375 to 0.09375
- contract_matrix: bfloat16 [14336, 3584], P('ts'), may hold values from -0.046875 to 0.046875
Outputs:
- token_grad: bfloat16 [8, 2048, 3584], P('dp', 'ts')
- gate_grad: bfloat16 [3584, 14336], P('dp', 'ts')
- up_grad: bfloat16 [3584, 14336], P('dp', 'ts')
- down_grad: bfloat16 [14336, 3584], P('ts', 'dp')
Inputs may be any that keep to these rules, and one draw needn't show every extreme that they name: `kept_locations`: for each sequence, 256 distinct positions in increasing order; each aligned block of 64 positions holds at most 32 of them, and in every sequence one block holds exactly 32.
All inputs are finite; a program needn't handle non-finite values.
Results may differ from a plain program's by a relative error of at most 0.023.
Values may be sent and summed in bfloat16 or wider, within the bound.
A program may use at most 128 MiB of HBM per device.

v0:
```python
import math

import jax
import jax.numpy as jnp
from jax import lax
from jax.sharding import PartitionSpec as P

epsilon = 1e-06
gelu_scale = math.sqrt(2.0 / math.pi)


def gelu_pair(pre_act):
    cubic = pre_act + 0.044715 * pre_act * pre_act * pre_act
    tanh_part = jnp.tanh(gelu_scale * cubic)
    gelu_out = 0.5 * pre_act * (1.0 + tanh_part)
    slope_out = 0.5 * (1.0 + tanh_part) + 0.5 * pre_act * (
        1.0 - tanh_part * tanh_part
    ) * gelu_scale * (1.0 + 3.0 * 0.044715 * pre_act * pre_act)
    return (gelu_out, slope_out)


def norm_backward(row_data, summed_grad, summed_dot, prenormal_scaling, scorer_matrix):
    row_f = row_data.astype(jnp.float32)
    inv_rms = lax.rsqrt(jnp.mean(row_f * row_f, axis=1, keepdims=True) + epsilon)
    unit_rows = row_f * inv_rms
    weight = jax.nn.sigmoid(jnp.dot(row_data, scorer_matrix, preferred_element_type=jnp.float32))
    logit_grad = (1.0 - weight) * summed_dot
    gained = summed_grad * prenormal_scaling.astype(jnp.float32)
    row_grad = inv_rms * (gained - unit_rows * jnp.mean(gained * unit_rows, axis=1, keepdims=True))
    return row_grad + logit_grad[:, None] * scorer_matrix.astype(jnp.float32)


def local(
    block_activity,
    result_cotangent,
    kept_locations,
    prenormal_scaling,
    scorer_matrix,
    switch_matrix,
    expand_matrix,
    contract_matrix,
):
    ts_width = lax.axis_size("ts")
    my_index = lax.axis_index("ts")
    local_tokens = block_activity.shape[1]
    model_width = block_activity.shape[2]
    keeper_limit = kept_locations.shape[1]
    slot_most = local_tokens // 2
    hidden_width = switch_matrix.shape[1]
    factor = (lax.axis_size("dp") * keeper_limit) ** (-0.5)
    kept_entries = kept_locations[0]
    holder = kept_entries // local_tokens
    local_pos = kept_entries - holder * local_tokens
    first_slot = jnp.sum((holder < my_index).astype(jnp.int32))
    own_count = jnp.sum((holder == my_index).astype(jnp.int32))
    padded_local = jnp.concatenate([local_pos, jnp.zeros((slot_most,), jnp.int32)])
    own_index = lax.dynamic_slice_in_dim(padded_local, first_slot, slot_most)
    own_valid = (jnp.arange(slot_most) < own_count)[:, None]
    own_rows = jnp.where(
        own_valid, jnp.take(block_activity[0], own_index, axis=0), jnp.zeros((), jnp.bfloat16)
    )
    own_grads = jnp.where(
        own_valid, jnp.take(result_cotangent[0], own_index, axis=0), jnp.zeros((), jnp.bfloat16)
    )
    holder_start = jnp.sum((holder[None, :] < holder[:, None]).astype(jnp.int32), axis=1)
    padded_pos = holder * slot_most + jnp.arange(keeper_limit, dtype=jnp.int32) - holder_start
    all_rows, all_grads = (
        lax.all_gather(own_rows, "ts", axis=0, tiled=True),
        lax.all_gather(own_grads, "ts", axis=0, tiled=True),
    )
    row_data = jnp.take(all_rows, padded_pos, axis=0)
    grad_data = jnp.take(all_grads, padded_pos, axis=0)
    row_f = row_data.astype(jnp.float32)
    inv_rms = lax.rsqrt(jnp.mean(row_f * row_f, axis=1, keepdims=True) + epsilon)
    normed = (row_f * inv_rms * prenormal_scaling.astype(jnp.float32)).astype(jnp.bfloat16)
    weight = jax.nn.sigmoid(jnp.dot(row_data, scorer_matrix, preferred_element_type=jnp.float32))
    pre_gate = jnp.dot(normed, switch_matrix, preferred_element_type=jnp.float32)
    pre_up = jnp.dot(normed, expand_matrix, preferred_element_type=jnp.float32)
    gelu_out, slope_out = gelu_pair(pre_gate)
    hidden = (gelu_out * pre_up).astype(jnp.bfloat16)
    scaled = (weight[:, None] * grad_data.astype(jnp.float32)).astype(jnp.bfloat16)
    hidden_grad = jnp.einsum(
        "cd,fd->cf", scaled, contract_matrix, preferred_element_type=jnp.float32
    )
    gate_in = (hidden_grad * pre_up * slope_out).astype(jnp.bfloat16)
    up_in = (hidden_grad * gelu_out).astype(jnp.bfloat16)
    dot_part = jnp.sum(hidden.astype(jnp.float32) * hidden_grad, axis=1)
    normed_term = jnp.einsum(
        "cf,df->cd", gate_in, switch_matrix, preferred_element_type=jnp.float32
    )
    normed_term = normed_term + jnp.einsum(
        "cf,df->cd", up_in, expand_matrix, preferred_element_type=jnp.float32
    )
    gate_term = jnp.einsum("cd,cf->df", normed, gate_in, preferred_element_type=jnp.float32)
    up_term = jnp.einsum("cd,cf->df", normed, up_in, preferred_element_type=jnp.float32)
    down_term = jnp.einsum("cd,cf->df", scaled, hidden, preferred_element_type=jnp.float32)
    summed_weights = lax.psum_scatter(
        (factor * jnp.concatenate([gate_term, up_term, down_term], axis=1)).astype(jnp.bfloat16),
        "dp",
        scatter_dimension=0,
        tiled=True,
    ).astype(jnp.float32)
    gate_grad = summed_weights[:, :hidden_width].astype(jnp.bfloat16)
    up_grad = summed_weights[:, hidden_width : 2 * hidden_width].astype(jnp.bfloat16)
    down_grad = summed_weights[:, 2 * hidden_width :].T.astype(jnp.bfloat16)
    term_pad = (
        jnp.zeros((ts_width * slot_most, model_width), jnp.float32).at[padded_pos].set(normed_term)
    )
    dot_pad = jnp.zeros((ts_width * slot_most,), jnp.float32).at[padded_pos].set(dot_part)
    own_term, own_dot = (
        lax.psum_scatter(
            term_pad.astype(jnp.bfloat16), "ts", scatter_dimension=0, tiled=True
        ).astype(jnp.float32),
        lax.psum_scatter(
            dot_pad.astype(jnp.bfloat16), "ts", scatter_dimension=0, tiled=True
        ).astype(jnp.float32),
    )
    row_grad = norm_backward(own_rows, own_term, own_dot, prenormal_scaling, scorer_matrix)
    placed = jnp.where(own_valid, row_grad, 0.0)
    token_grad = jnp.zeros((local_tokens, model_width), jnp.float32).at[own_index].add(placed)
    token_grad = token_grad.astype(jnp.bfloat16)[None]
    return (token_grad, gate_grad, up_grad, down_grad)


def solution(mesh):
    in_specs = (
        P("dp", "ts", None),
        P("dp", "ts", None),
        P("dp", None),
        P(),
        P(),
        P(None, "ts"),
        P(None, "ts"),
        P("ts", None),
    )
    out_specs = (P("dp", "ts", None), P("dp", "ts"), P("dp", "ts"), P("ts", "dp"))
    return jax.shard_map(local, mesh=mesh, in_specs=in_specs, out_specs=out_specs, check_vma=False)
```

profile of v0, /device:TPU:2, one launch (start us, length us, event | category | flops | bytes accessed | tf_op | source)
XLA Modules:
  0.0 538.2 jit_solution(17822663819450770305)
XLA Ops:
  7.3 0.8 multiply_subtract_fusion
  11.4 2.0 gather_fusion
  13.4 0.9 fusion.21
  14.4 2.0 gather_fusion.2
  17.6 93.2 %all-gather.3.cloned.1.call-done = bf16[1024,3584]{1,0:T(8,128)(2,1)} async-done(((bf16[32,3584]{1,0:T(8,128)(2,1)}), bf16[1024,3584]{1,0:T(8,128)(2,1)}) %all-gather.3.cloned.1.call-update) | async-done | bytes 7340048 | tf_op jit(solution)/shard_map/all_gather | solution.py:68
  110.8 8.8 %gather_fusion.1 = bf16[256,3584]{1,0:T(8,128)(2,1)} fusion(bf16[1024,3584]{1,0:T(8,128)(2,1)} %all-gather.3.cloned.1.call-done, s32[1024]{0:T(1024)S(1)} %pad_clamp_fusion), kind=kCustom, calls=%fused_computation.1.clone | custom fusion | bytes 3671040 | tf_op jit(solution)/shard_map/jit(_take)/gather | solution.py:71
  119.6 2.3 fusion.3
  121.9 2.2 fusion.42
  124.1 3.9 fusion.51
  128.0 1.9 fusion.49
  130.0 74.4 %all-gather.5.cloned.1.call-done = bf16[1024,3584]{1,0:T(8,128)(2,1)} async-done(((bf16[32,3584]{1,0:T(8,128)(2,1)}), bf16[1024,3584]{1,0:T(8,128)(2,1)}) %all-gather.5.cloned.1.call-update) | async-done | bytes 7340048 | tf_op jit(solution)/shard_map/all_gather | solution.py:69
  204.4 8.8 %gather_fusion.3 = bf16[256,3584]{1,0:T(8,128)(2,1)} fusion(bf16[1024,3584]{1,0:T(8,128)(2,1)} %all-gather.5.cloned.1.call-done, s32[1024]{0:T(1024)S(1)} %pad_clamp_fusion), kind=kCustom, calls=%fused_computation.3.clone | custom fusion | bytes 3671040 | tf_op jit(solution)/shard_map/jit(_take)/gather | solution.py:72
  213.2 4.9 multiply_reduce_fusion
  218.1 1.1 fusion.54
  219.3 0.8 copy-done.5
  220.1 3.0 convolution_add_fusion
  223.1 10.2 %scatter_custom_fusion = f32[1024,3584]{1,0:T(8,128)} fusion(s32[256]{0:T(256)S(1)} %bitcast.55, f32[256,3584]{1,0:T(8,128)} %convolution_add_fusion, f32[]{:T(128)} %constant.36.clone.1), kind=kCustom, calls=%fused_computation.9 | custom fusion | bytes 14680576 | tf_op jit(solution)/shard_map/scatter | solution.py:107
  233.3 9.0 %convert_element_type.79 = bf16[1024,3584]{1,0:T(8,128)(2,1)} convert(f32[1024,3584]{1,0:T(8,128)} %scatter_custom_fusion) | non-fusion elementwise | flops 3670016 | bytes 22020096 | tf_op jit(solution)/shard_map/convert_element_type | solution.py:112
  243.2 2.8 fusion.43
  246.1 1.2 fusion.47
  247.2 1.2 fusion.45
  248.4 6.7 %fusion = bf16[3584,1344]{0,1:T(8,128)(2,1)} fusion(f32[3584,448]{0,1:T(8,128)S(1)} %fusion.43, f32[3584,448]{0,1:T(8,128)S(1)} %fusion.47, f32[3584,448]{0,1:T(8,128)S(1)} %fusion.45), kind=kLoop, calls=%fused_computation.8 | loop fusion | flops 19267584 | bytes 28901376 | tf_op jit(solution)/shard_map/convert_element_type | solution.py:98
  255.1 13.4 %copy.20 = bf16[3584,1344]{1,0:T(8,128)(2,1)} copy(bf16[3584,1344]{0,1:T(8,128)(2,1)} %fusion) | data formatting | bytes 19267584
  270.5 1.4 scatter_custom_fusion.1
  271.9 71.9 %all-reduce.1 = bf16[1024]{0:T(1024)(128)(2,1)S(1)} all-reduce(bf16[1024]{0:T(1024)(128)(2,1)S(1)} %convert_element_type.83), channel_id=3, replica_groups=mesh['dp'=8,'ts'=32] {'ts'}, use_global_device_ids=true, to_apply=%region_10.13.clone | all-reduce | flops 1024 | bytes 4096
  344.0 121.6 %reduce-scatter.5.cloned.1.call-done = bf16[32,3584]{1,0:T(8,128)(2,1)} async-done(((bf16[1024,3584]{1,0:T(8,128)(2,1)}), bf16[32,3584]{1,0:T(8,128)(2,1)}) %reduce-scatter.5.cloned.1.call-update) | async-done | bytes 229392 | tf_op jit(solution)/shard_map/reduce_scatter | solution.py:111
  465.5 1.2 fusion.14
  466.7 2.9 scatter_custom_fusion.2
  469.6 2.0 convert_bitcast_fusion
  471.6 55.4 %reduce-scatter.7.cloned.1.call-done = bf16[448,1344]{1,0:T(8,128)(2,1)} async-done(((bf16[3584,1344]{1,0:T(8,128)(2,1)}), bf16[448,1344]{1,0:T(8,128)(2,1)}) %reduce-scatter.7.cloned.1.call-update) | async-done | bytes 1204240
  527.1 2.6 fusion.53
  529.7 2.0 copy.24
  (52 shorter events, 5.0 us)
Async XLA Ops:
  7.2 120.9 %copy-start = (bf16[3584,448]{0,1:T(8,128)(2,1)S(1)}, bf16[3584,448]{0,1:T(8,128)(2,1)}, u32[]{:S(2)}) copy-start(bf16[3584,448]{0,1:T(8,128)(2,1)} %param.17) | copy-start | bytes 9633796
  7.2 10.2 %copy-start.10 = (s32[1,256]{1,0:T(1,128)S(1)}, s32[1,256]{1,0:T(1,128)}, u32[]{:S(2)}) copy-start(s32[1,256]{1,0:T(1,128)} %param.14) | copy-start | bytes 3076
  7.2 10.1 %copy-start.11 = (bf16[3584]{0:T(1024)(128)(2,1)S(1)}, bf16[3584]{0:T(1024)(128)(2,1)}, u32[]{:S(2)}) copy-start(bf16[3584]{0:T(1024)(128)(2,1)} %param.15) | copy-start | bytes 21508
  7.2 10.1 %copy-start.9 = (bf16[3584]{0:T(1024)(128)(2,1)S(1)}, bf16[3584]{0:T(1024)(128)(2,1)}, u32[]{:S(2)}) copy-start(bf16[3584]{0:T(1024)(128)(2,1)} %param.16) | copy-start | bytes 21508
  7.2 103.6 %all-gather.3.cloned.1.call-start = ((), (), s32[]{:S(2)}) async-start(), calls=%async_computation.2 | async-start | bytes 7569408 | tf_op jit(solution)/shard_map/all_gather | solution.py:68
  14.4 190.0 %all-gather.5.cloned.1.call-start = ((), (), s32[]{:S(2)}) async-start(), calls=%async_computation.3 | async-start | bytes 7569408 | tf_op jit(solution)/shard_map/all_gather | solution.py:69
  17.2 448.3 %reduce-scatter.5.cloned.1.call-start = ((), (), s32[]{:S(2)}) async-start(), calls=%async_computation.4 | async-start | bytes 7569408 | tf_op jit(solution)/shard_map/reduce_scatter | solution.py:111
  119.6 4.5 copy-start.2
  218.1 1.1 copy-start.6
  218.1 2.0 copy-start.5
  242.3 0.9 copy-start.8
  242.3 284.7 %reduce-scatter.7.cloned.1.call-start = ((), (), s32[]{:S(2)}) async-start(), calls=%async_computation.5 | async-start | bytes 11354112
  243.2 2.8 copy-start.3
  243.2 2.8 copy-start.7
  268.6 0.7 copy-start.12
  268.6 75.3 %copy-start.4 = (bf16[32,3584]{1,0:T(8,128)(2,1)S(1)}, bf16[32,3584]{1,0:T(8,128)(2,1)}, u32[]{:S(2)}) copy-start(bf16[32,3584]{1,0:T(8,128)(2,1)} %get-tuple-element.25) | copy-start | bytes 688132
  466.7 65.0 %copy-start.1 = (bf16[3584,448]{0,1:T(8,128)(2,1)S(1)}, bf16[3584,448]{0,1:T(8,128)(2,1)}, u32[]{:S(2)}) copy-start(bf16[3584,448]{0,1:T(8,128)(2,1)} %param.17) | copy-start | bytes 9633796
Sparse Core Ops, SparseCore 0:
  14.5 96.2 all-gather.2
  114.0 90.3 all-gather.4
  242.4 223.0 reduce-scatter.4
  468.1 58.8 reduce-scatter.6
where the time goes:
time: 542 us; the launch traced here: 538 us
  waiting for transfers between devices  345 us (64%)
  blocking collectives  71.9 us (13%)
  local copies, waits for them, and re-layouts  54 us (10%)
  other arithmetic  28.3 us (5%)
  matrix products  22.3 us (4%)
  between operations  16.6 us (3%)
    reduce_scatter x1, waiting for transfers between devices, local(): lax.psum_scatter(term_pad.astype(jnp.bfloat16), 'ts', scatter_dimension=0...  122 us
    all_gather x1, waiting for transfers between devices, local(): lax.all_gather(own_rows, 'ts', axis=0, tiled=True)  93.2 us
    all_gather x1, waiting for transfers between devices, local(): lax.all_gather(own_grads, 'ts', axis=0, tiled=True)  74.4 us
    unnamed x1, blocking collectives  71.9 us
    unnamed x5, waiting for transfers between devices  55.5 us
    unnamed x30, local copies, waits for them, and re-layouts  18.2 us
  transfers between devices with their start and end apart: 4, of which 4 were waited for; matrix products, arithmetic and copies ran while one was open for 10% of the time, Pallas kernels for 0%

commit v1 on v0

v1 whole, which is shorter than its diff:
```python
import functools
import math

import jax
import jax.numpy as jnp
from jax import lax
from jax.experimental import pallas as pl
from jax.experimental.pallas import tpu as pltpu
from jax.sharding import PartitionSpec as P

MESH = pl.DeviceIdType.MESH
NY = 4
Z_STEPS = (0, -1, 1, -2, 2, -3, 3, 4)


def gather_kernel(n_ts, block, kept_ref, slots_ref, full_ref, landed, wide, p1_send, p1_recv, send_sem, recv_sem):
    nz = n_ts // NY
    me = lax.axis_index("ts")
    z, y = me // NY, lax.rem(me, NY)
    rows, width = full_ref.shape[2], full_ref.shape[3]
    lanes = wide.shape[2]
    half = width // 2

    def node(dz, dy):
        return lax.rem(z + dz + nz, nz) * NY + lax.rem(y + dy + NY, NY)

    barrier = pltpu.get_barrier_semaphore()

    @pl.loop(1, n_ts)
    def _(step):
        pl.semaphore_signal(barrier, inc=1, device_id={"ts": lax.rem(me + step, n_ts)}, device_id_type=MESH)

    pl.semaphore_wait(barrier, n_ts - 1)

    @pl.loop(1, n_ts)
    def _(step):
        to = lax.rem(me + step, n_ts)
        pltpu.make_async_remote_copy(
            slots_ref.at[to], landed.at[me], p1_send.at[step], p1_recv.at[step],
            device_id={"ts": to}, device_id_type=MESH,
        ).start()

    landed[me] = slots_ref[me]

    @pl.loop(1, n_ts)
    def _(step):
        to = lax.rem(me + step, n_ts)
        source = lax.rem(me - step + n_ts, n_ts)
        pltpu.make_async_remote_copy(
            slots_ref.at[to], landed.at[source], p1_send.at[step], p1_recv.at[step],
            device_id={"ts": to}, device_id_type=MESH,
        ).wait()

    for k in range(rows):
        holder = kept_ref[0, n_ts * k + me] // block
        wide[k] = landed[holder].astype(jnp.float32)
    tiles = width // lanes
    for part in range(2):
        for t in range(tiles):
            full_ref[part, me, :, t * lanes:(t + 1) * lanes] = wide[:, part * tiles + t, :].astype(jnp.bfloat16)

    pending = []

    def send(index, ref, to):
        copy = pltpu.make_async_remote_copy(
            ref, ref, send_sem.at[index], recv_sem.at[index], device_id={"ts": to}, device_id_type=MESH)
        copy.start()
        pending.append(copy)

    def arrive(index, ref):
        pltpu.make_async_remote_copy(
            ref, ref, send_sem.at[index], recv_sem.at[index], device_id={"ts": me}, device_id_type=MESH).wait_recv()

    def piece(part, n):
        return full_ref.at[part, n]

    def piece_half(part, n, which):
        return full_ref.at[part, n, :, pl.ds(which * half, half)]

    def group(dz):
        return full_ref.at[1, pl.ds(lax.rem(z + dz + nz, nz) * NY, NY)]

    def group_half(dz, which):
        return full_ref.at[1, pl.ds(lax.rem(z + dz + nz, nz) * NY + which * (NY // 2), NY // 2)]

    up, down, left, right = node(1, 0), node(-1, 0), node(0, -1), node(0, 1)
    B1, A1, B2, A2, A3 = 0, 4, 12, 20, 36

    send(B1 + 0, piece(1, me), right)
    send(B1 + 1, piece(1, me), left)
    send(A1 + 0, piece(0, me), up)
    send(A1 + 1, piece(0, me), down)

    def spread(j):
        dz = Z_STEPS[j]
        send(A2 + 2 * j, piece(0, node(dz, 0)), right)
        send(A2 + 2 * j + 1, piece(0, node(dz, 0)), left)

    def relay(j):
        dz = Z_STEPS[j]
        arrive(A2 + 2 * j, piece(0, node(dz, -1)))
        send(A3 + 2 * j, piece_half(0, node(dz, -1), 0), right)
        arrive(A2 + 2 * j + 1, piece(0, node(dz, 1)))
        send(A3 + 2 * j + 1, piece_half(0, node(dz, 1), 1), left)

    def along(s):
        if s < 4:
            arrive(A1 + 2 * (s - 1), piece(0, node(-s, 0)))
            if s < 3:
                send(A1 + 2 * s, piece(0, node(-s, 0)), up)
            else:
                send(A1 + 6, piece_half(0, node(-3, 0), 0), up)
            arrive(A1 + 2 * (s - 1) + 1, piece(0, node(s, 0)))
            if s < 3:
                send(A1 + 2 * s + 1, piece(0, node(s, 0)), down)
            else:
                send(A1 + 7, piece_half(0, node(3, 0), 1), down)
            spread(2 * s - 1)
            spread(2 * s)
        else:
            arrive(A1 + 6, piece_half(0, node(-4, 0), 0))
            arrive(A1 + 7, piece_half(0, node(4, 0), 1))
            spread(7)

    def groups(s):
        if s < 4:
            arrive(B2 + 2 * (s - 1), group(-s))
            if s < 3:
                send(B2 + 2 * s, group(-s), up)
            else:
                send(B2 + 6, group_half(-3, 0), up)
            arrive(B2 + 2 * (s - 1) + 1, group(s))
            if s < 3:
                send(B2 + 2 * s + 1, group(s), down)
            else:
                send(B2 + 7, group_half(3, 1), down)
        else:
            arrive(B2 + 6, group_half(-4, 0))
            arrive(B2 + 7, group_half(4, 1))

    spread(0)
    arrive(B1 + 0, piece(1, node(0, -1)))
    send(B1 + 2, piece_half(1, node(0, -1), 0), right)
    arrive(B1 + 1, piece(1, node(0, 1)))
    send(B1 + 3, piece_half(1, node(0, 1), 1), left)
    along(1)
    arrive(B1 + 2, piece_half(1, node(0, -2), 0))
    arrive(B1 + 3, piece_half(1, node(0, 2), 1))
    send(B2 + 0, group(0), up)
    send(B2 + 1, group(0), down)
    along(2)
    relay(0)
    along(3)
    relay(1)
    relay(2)
    groups(1)
    along(4)
    relay(3)
    relay(4)
    groups(2)
    relay(5)
    relay(6)
    relay(7)
    groups(3)
    for j in range(8):
        arrive(A3 + 2 * j, piece_half(0, node(Z_STEPS[j], -2), 0))
        arrive(A3 + 2 * j + 1, piece_half(0, node(Z_STEPS[j], 2), 1))
    groups(4)
    for copy in pending:
        copy.wait_send()


def gather_rows(kept, slots, n_ts, block):
    tiles = slots.shape[1] // 2
    width = tiles * slots.shape[2]
    rows = kept.shape[1] // n_ts
    return pl.pallas_call(
        functools.partial(gather_kernel, n_ts, block),
        out_shape=jax.ShapeDtypeStruct((2, n_ts, rows, width), jnp.bfloat16),
        in_specs=[pl.BlockSpec(memory_space=pltpu.SMEM), pl.BlockSpec(memory_space=pltpu.VMEM)],
        out_specs=pl.BlockSpec(memory_space=pltpu.VMEM),
        scratch_shapes=[
            pltpu.VMEM(slots.shape, jnp.bfloat16),
            pltpu.VMEM((rows,) + slots.shape[1:], jnp.float32),
            pltpu.SemaphoreType.DMA((n_ts,)),
            pltpu.SemaphoreType.DMA((n_ts,)),
            pltpu.SemaphoreType.DMA((52,)),
            pltpu.SemaphoreType.DMA((52,)),
        ],
        compiler_params=pltpu.CompilerParams(
            collective_id=0, has_side_effects=True, vmem_limit_bytes=24 * 1024 * 1024),
        name="gather_rows",
    )(kept, slots)


def reduce_weights(parts):
    return lax.psum_scatter(parts, "dp", scatter_dimension=0, tiled=True)


epsilon = 1e-06
gelu_scale = math.sqrt(2.0 / math.pi)


def gelu_pair(pre_act):
    cubic = pre_act + 0.044715 * pre_act * pre_act * pre_act
    tanh_part = jnp.tanh(gelu_scale * cubic)
    gelu_out = 0.5 * pre_act * (1.0 + tanh_part)
    slope_out = 0.5 * (1.0 + tanh_part) + 0.5 * pre_act * (
        1.0 - tanh_part * tanh_part
    ) * gelu_scale * (1.0 + 3.0 * 0.044715 * pre_act * pre_act)
    return (gelu_out, slope_out)


def norm_backward(row_data, summed_grad, summed_dot, prenormal_scaling, scorer_matrix):
    row_f = row_data.astype(jnp.float32)
    inv_rms = lax.rsqrt(jnp.mean(row_f * row_f, axis=1, keepdims=True) + epsilon)
    unit_rows = row_f * inv_rms
    weight = jax.nn.sigmoid(jnp.dot(row_data, scorer_matrix, preferred_element_type=jnp.float32))
    logit_grad = (1.0 - weight) * summed_dot
    gained = summed_grad * prenormal_scaling.astype(jnp.float32)
    row_grad = inv_rms * (gained - unit_rows * jnp.mean(gained * unit_rows, axis=1, keepdims=True))
    return row_grad + logit_grad[:, None] * scorer_matrix.astype(jnp.float32)


def local(
    block_activity, result_cotangent, kept_locations, prenormal_scaling, scorer_matrix,
    switch_matrix, expand_matrix, contract_matrix,
):
    n_ts = lax.axis_size("ts")
    me = lax.axis_index("ts")
    n_dp = lax.axis_size("dp")
    local_tokens = block_activity.shape[1]
    model_width = block_activity.shape[2]
    cap = kept_locations.shape[1]
    hidden_width = switch_matrix.shape[1]
    factor = (n_dp * cap) ** (-0.5)
    kept = kept_locations[0]
    first = jnp.sum((kept < me * local_tokens).astype(jnp.int32))
    count = jnp.sum((kept // local_tokens == me).astype(jnp.int32))
    classes = jnp.arange(n_ts, dtype=jnp.int32)
    ranks = first + lax.rem(classes - lax.rem(first, n_ts) + n_ts, n_ts)
    own_valid = ranks < first + count
    own_index = jnp.clip(jnp.take(kept, jnp.minimum(ranks, cap - 1)) - me * local_tokens, 0, local_tokens - 1)
    own_rows = jnp.take(block_activity[0], own_index, axis=0)
    own_grads = jnp.take(result_cotangent[0], own_index, axis=0)
    slots = jnp.concatenate([own_rows, own_grads], axis=1).reshape(n_ts, -1, 128)
    full = gather_rows(kept_locations, slots, n_ts, local_tokens)
    row_data = full[0].reshape(cap, model_width)
    grad_data = full[1].reshape(cap, model_width)

    row_f = row_data.astype(jnp.float32)
    inv_rms = lax.rsqrt(jnp.mean(row_f * row_f, axis=1, keepdims=True) + epsilon)
    normed = (row_f * inv_rms * prenormal_scaling.astype(jnp.float32)).astype(jnp.bfloat16)
    weight = jax.nn.sigmoid(jnp.dot(row_data, scorer_matrix, preferred_element_type=jnp.float32))
    pre_gate = jnp.dot(normed, switch_matrix, preferred_element_type=jnp.float32)
    pre_up = jnp.dot(normed, expand_matrix, preferred_element_type=jnp.float32)
    gelu_out, slope_out = gelu_pair(pre_gate)
    hidden = (gelu_out * pre_up).astype(jnp.bfloat16)
    scaled = (weight[:, None] * grad_data.astype(jnp.float32)).astype(jnp.bfloat16)
    hidden_grad = jnp.einsum("cd,fd->cf", scaled, contract_matrix, preferred_element_type=jnp.float32)
    gate_in = (hidden_grad * pre_up * slope_out).astype(jnp.bfloat16)
    up_in = (hidden_grad * gelu_out).astype(jnp.bfloat16)
    dot_part = jnp.sum(hidden.astype(jnp.float32) * hidden_grad, axis=1)
    normed_term = jnp.einsum("cf,df->cd", gate_in, switch_matrix, preferred_element_type=jnp.float32)
    normed_term = normed_term + jnp.einsum("cf,df->cd", up_in, expand_matrix, preferred_element_type=jnp.float32)
    term = jnp.concatenate(
        [normed_term, jnp.broadcast_to(dot_part[:, None], (cap, 128))], axis=1).astype(jnp.bfloat16)
    own_sum = lax.psum_scatter(term, "ts", scatter_dimension=0, tiled=True)
    gate_term = jnp.einsum("cd,cf->df", normed, gate_in, preferred_element_type=jnp.float32)
    up_term = jnp.einsum("cd,cf->df", normed, up_in, preferred_element_type=jnp.float32)
    down_term = jnp.einsum("cd,cf->df", scaled, hidden, preferred_element_type=jnp.float32)
    parts = (factor * jnp.concatenate([gate_term, up_term, down_term], axis=1)).astype(jnp.bfloat16)
    summed_weights = reduce_weights(parts)
    gate_grad = summed_weights[:, :hidden_width]
    up_grad = summed_weights[:, hidden_width : 2 * hidden_width]
    down_grad = summed_weights[:, 2 * hidden_width :].T

    class_holder = jnp.take(kept.reshape(-1, n_ts), me, axis=1) // local_tokens
    pick = jnp.argmax(class_holder[None, :] == classes[:, None], axis=1)
    back = lax.all_to_all(jnp.take(own_sum, pick, axis=0), "ts", split_axis=0, concat_axis=0, tiled=True)
    own_term = back[:, :model_width].astype(jnp.float32)
    own_dot = back[:, model_width].astype(jnp.float32)
    row_grad = norm_backward(own_rows, own_term, own_dot, prenormal_scaling, scorer_matrix)
    row_grad = jnp.where(own_valid[:, None], row_grad, 0.0).astype(jnp.bfloat16)
    place = (jnp.arange(local_tokens)[:, None] == own_index[None, :]) & own_valid[None, :]
    token_grad = jnp.dot(place.astype(jnp.bfloat16), row_grad, preferred_element_type=jnp.float32)
    return (token_grad.astype(jnp.bfloat16)[None], gate_grad, up_grad, down_grad)


def solution(mesh):
    in_specs = (
        P("dp", "ts", None), P("dp", "ts", None), P("dp", None), P(), P(),
        P(None, "ts"), P(None, "ts"), P("ts", None),
    )
    out_specs = (P("dp", "ts", None), P("dp", "ts"), P("dp", "ts"), P("ts", "dp"))
    return jax.shard_map(local, mesh=mesh, in_specs=in_specs, out_specs=out_specs, check_vma=False)
```

time: 542 us -> 285 us (0.53)
  waiting for transfers between devices: 345 us -> 133 us
  blocking collectives: 71.9 us -> 0 us
  Pallas kernels: 0 us -> 57.9 us
  local copies, waits for them, and re-layouts: 54 us -> 35.5 us
  other arithmetic: 28.3 us -> 17 us
  matrix products: 22.3 us -> 15.2 us
    all_gather x2 -> x0, waiting for transfers between devices: 168 us -> none  [the longest x1 93.2 us: local(): lax.all_gather(own_rows, 'ts', axis=0, tiled=True)]
    reduce_scatter x1 -> x0, waiting for transfers between devices: 122 us -> none  [local(): lax.psum_scatter(term_pad.astype(jnp.bfloat16), 'ts', scatter_dimension=0...]
    unnamed x1 -> x0, blocking collectives: 71.9 us -> none
    unnamed x5 -> x4, waiting for transfers between devices: 55.5 us -> 124 us
    pallas_call x0 -> x1, Pallas kernels: none -> 57.9 us  [gather_rows(): pl.pallas_call(functools.partial(gather_kernel, n_ts, block), out_shape=j...]
    gather x4, local copies, waits for them, and re-layouts: 21.6 us -> 6.81 us  [the longest x1 2.67 us: local(): own_rows = jnp.take(block_activity[0], own_index, axis=0)]
    scatter x2 -> x0, local copies, waits for them, and re-layouts: 11.6 us -> none  [the longest x1 10.2 us: local(): jnp.zeros((ts_width * slot_most, model_width), jnp.float32).at[padded_pos]]
    all_to_all x0 -> x1, waiting for transfers between devices: none -> 9.06 us  [local(): lax.all_to_all(jnp.take(own_sum, pick, axis=0), 'ts', split_axis=0, conca...]
  transfers between devices with their start and end apart: 4 -> 3, of which waited for: 4 -> 2; matrix products, arithmetic and copies ran while one was open for 10% -> 13% of each run, Pallas kernels for 0% -> 0%
where the time goes in v1:
time: 285 us; the launch traced here: 284 us
  waiting for transfers between devices  133 us (47%)
  Pallas kernels  57.9 us (20%)
  local copies, waits for them, and re-layouts  35.5 us (12%)
  between operations  20.2 us (7%)
  other arithmetic  17 us (6%)
  matrix products  15.2 us (5%)
  starting transfers between devices  5.61 us (2%)
    unnamed x4, waiting for transfers between devices  124 us
    pallas_call x1, Pallas kernels, gather_rows(): pl.pallas_call(functools.partial(gather_kernel, n_ts, block), out_shape=j...  57.9 us
    unnamed x41, local copies, waits for them, and re-layouts  25.2 us
    all_to_all x1, waiting for transfers between devices, local(): lax.all_to_all(jnp.take(own_sum, pick, axis=0), 'ts', split_axis=0, conca...  9.06 us
    convert_element_type x1, other arithmetic, local(): (factor * jnp.concatenate([gate_term, up_term, down_term], axis=1)).astyp...  6.86 us
  transfers between devices with their start and end apart: 3, of which 2 were waited for; matrix products, arithmetic and copies ran while one was open for 13% of the time, Pallas kernels for 0%

profile of v1, /device:TPU:2, one launch (start us, length us, event | category | flops | bytes accessed | tf_op | source)
XLA Modules:
  0.0 284.3 jit_solution(10944461460744109474)
XLA Ops:
  8.1 1.6 fusion.47
  12.4 1.5 gather_fusion
  13.9 0.7 compare_and_fusion
  16.0 2.0 gather_fusion.3
  18.0 2.7 gather_fusion.2
  20.8 1.2 fusion.25
  22.1 57.9 %gather_rows.1 = bf16[2,32,8,3584]{3,2,1,0:T(8,128)(2,1)S(1)} custom-call(s32[1,256]{1,0:T(1,128)S(1)} %copy-done.2, bf16[32,56,128]{2,1,0:T(8,128)(2,1)S(1)} %bitcast.67), custom_call_target="tpu_custom_call" | custom-call | tf_op jit(solution)/shard_map/gather_rows/pallas_call | solution.py:177
  80.4 1.3 copy-done.3
  82.5 2.8 fusion.58
  85.3 0.8 copy-done.6
  86.1 1.1 fusion.59
  87.2 0.8 copy-done.13
  88.0 2.1 multiply_reduce_fusion.1
  90.1 1.1 fusion.61
  91.2 1.2 fusion.1
  92.6 1.4 pad_maximum_fusion
  94.3 2.8 fusion.57
  97.1 1.1 fusion.15
  98.2 1.1 fusion.56
  99.4 6.9 %fusion = bf16[3584,1344]{0,1:T(8,128)(2,1)} fusion(f32[3584,448]{0,1:T(8,128)S(1)} %fusion.15, f32[3584,448]{0,1:T(8,128)S(1)} %fusion.57, f32[3584,448]{0,1:T(8,128)S(1)} %fusion.56), kind=kLoop, calls=%fused_computation.5 | loop fusion | flops 19267584 | bytes 28901376 | tf_op jit(solution)/shard_map/convert_element_type | solution.py:272
  106.2 13.6 %copy.30 = bf16[3584,1344]{1,0:T(8,128)(2,1)} copy(bf16[3584,1344]{0,1:T(8,128)(2,1)} %fusion) | data formatting | bytes 19267584
  123.1 123.8 %all-reduce.3.cloned.1.call-done = bf16[256,3712]{1,0:T(8,128)(2,1)} async-done(((bf16[256,3712]{1,0:T(8,128)(2,1)}), bf16[256,3712]{1,0:T(8,128)(2,1)}) %all-reduce.3.cloned.1.call-update) | async-done | bytes 1900560
  246.9 0.8 constant_dynamic-slice_fusion
  249.1 0.7 reduce.26
  249.8 0.9 reshape.276
  250.8 5.3 %all-to-all-start = ((bf16[32,2,1856]{2,1,0:T(2,128)(2,1)}), bf16[32,2,1856]{2,1,0:T(2,128)(2,1)}, u32[]{:S(2)}, u32[]{:S(2)}) async-start(bf16[32,2,1856]{2,1,0:T(2,128)(2,1)} %reshape.276), calls=%async_computation | async-start | bytes 491520 | tf_op jit(solution)/shard_map/all_to_all | solution.py:280
  258.5 9.1 %all-to-all-done = bf16[32,2,1856]{2,1,0:T(2,128)(2,1)} async-done(((bf16[32,2,1856]{2,1,0:T(2,128)(2,1)}), bf16[32,2,1856]{2,1,0:T(2,128)(2,1)}, u32[]{:S(2)}, u32[]{:S(2)}) %all-to-all-start) | async-done | bytes 237600 | tf_op jit(solution)/shard_map/all_to_all | solution.py:280
  267.5 2.0 reshape.277
  269.5 1.1 copy.39
  271.1 1.2 fusion.2
  272.2 2.6 fusion.60
  274.8 2.0 copy.36
  (68 shorter events, 9.1 us)
Async XLA Ops:
  8.0 74.5 %copy-start = (bf16[3584,448]{0,1:T(8,128)(2,1)S(1)}, bf16[3584,448]{0,1:T(8,128)(2,1)}, u32[]{:S(2)}) copy-start(bf16[3584,448]{0,1:T(8,128)(2,1)} %param.15) | copy-start | bytes 9633796
  8.0 238.9 %all-reduce.3.cloned.1.call-start = ((), (), s32[]{:S(2)}) async-start(), calls=%async_computation.3 | async-start | bytes 3801088
  12.4 9.7 %copy-start.2 = (s32[1,256]{1,0:T(1,128)S(1)}, s32[1,256]{1,0:T(1,128)}, u32[]{:S(2)}) copy-start(s32[1,256]{1,0:T(1,128)} %kept_ref.1) | copy-start | bytes 3076
  80.0 1.8 copy-start.3
  82.5 2.8 copy-start.4
  82.5 3.6 %copy-start.6 = (bf16[3584,448]{0,1:T(8,128)(2,1)S(1)}, bf16[3584,448]{0,1:T(8,128)(2,1)}, u32[]{:S(2)}) copy-start(bf16[3584,448]{0,1:T(8,128)(2,1)} %param.16) | copy-start | bytes 9633796
  86.1 1.9 copy-start.13
  90.1 1.2 copy-start.7
  90.1 1.2 copy-start.9
  92.5 1.8 copy-start.10
  94.0 3.0 %copy-start.11 = (bf16[256,448]{0,1:T(8,128)(2,1)S(1)}, bf16[256,448]{0,1:T(8,128)(2,1)}, u32[]{:S(2)}) copy-start(bf16[256,448]{0,1:T(8,128)(2,1)} %get-tuple-element.43) | copy-start | bytes 688132
  94.0 178.2 %reduce-scatter.4.cloned.1.call-start = ((), (), s32[]{:S(2)}) async-start(), calls=%async_computation.2 | async-start | bytes 11354112
  94.3 2.8 copy-start.5
  97.1 1.1 copy-start.8
  119.8 1.5 copy-start.14
  119.8 136.3 %copy-start.12 = (bf16[3584]{0:T(1024)(128)(2,1)S(1)}, bf16[3584]{0:T(1024)(128)(2,1)}, u32[]{:S(2)}) copy-start(bf16[3584]{0:T(1024)(128)(2,1)} %param.14) | copy-start | bytes 21508
  250.8 16.8 %all-to-all-start = ((bf16[32,2,1856]{2,1,0:T(2,128)(2,1)}), bf16[32,2,1856]{2,1,0:T(2,128)(2,1)}, u32[]{:S(2)}, u32[]{:S(2)}) async-start(bf16[32,2,1856]{2,1,0:T(2,128)(2,1)} %reshape.276), calls=%async_computation | async-start | bytes 491520 | tf_op jit(solution)/shard_map/all_to_all | solution.py:280
  256.1 20.7 %copy-start.1 = (bf16[3584,448]{0,1:T(8,128)(2,1)S(1)}, bf16[3584,448]{0,1:T(8,128)(2,1)}, u32[]{:S(2)}) copy-start(bf16[3584,448]{0,1:T(8,128)(2,1)} %param.15) | copy-start | bytes 9633796
Sparse Core Ops, SparseCore 0:
  94.1 152.7 all-reduce.2
Sparse Core Ops, SparseCore 1:
  119.9 59.8 reduce-scatter.3

commit v2 on v1

--- a/solution.py
+++ b/solution.py
@@ -193,8 +193,242 @@
     )(kept, slots)
 
 
-def reduce_weights(parts):
-    return lax.psum_scatter(parts, "dp", scatter_dimension=0, tiled=True)
+def reduce_kernel(
+    n_ts, n_dp, factor,
+    pick_ref, normed_ref, scaled_ref, acts_ref, term_ref, out_ref, back_ref,
+    pair, sib, x_first, x_last, y_first, y_last, y_sum, z_in, z_out, spread, rows_out, slots_out,
+    sib_send, sib_recv, x_send, x_recv, y_send, y_recv, z_send, z_recv, b_send, b_recv,
+):
+    nz = n_ts // NY
+    nx = n_dp // 2
+    me = lax.axis_index("ts")
+    z, y = me // NY, lax.rem(me, NY)
+    dp = lax.axis_index("dp")
+    x, core = dp // 2, lax.rem(dp, 2)
+    rows = sib.shape[1]
+    quarter = rows // 4
+    hidden = acts_ref.shape[1] // 3
+    pending = []
+
+    def node(dz, dy):
+        return lax.rem(z + dz + nz, nz) * NY + lax.rem(y + dy + NY, NY)
+
+    def chip(dx):
+        return lax.rem(x + dx + nx, nx) * 2 + core
+
+    barrier = pltpu.get_barrier_semaphore()
+
+    @pl.loop(1, n_ts)
+    def _(step):
+        pl.semaphore_signal(barrier, inc=1, device_id={"ts": lax.rem(me + step, n_ts)}, device_id_type=MESH)
+
+    for other in (x * 2 + 1 - core, chip(1), chip(-1)):
+        pl.semaphore_signal(barrier, inc=1, device_id={"dp": other}, device_id_type=MESH)
+    pl.semaphore_wait(barrier, n_ts - 1 + 3)
+
+    def copy_to(sems, index, src, dst, where):
+        return pltpu.make_async_remote_copy(
+            src, dst, sems[0].at[index], sems[1].at[index], device_id=where, device_id_type=MESH)
+
+    def send(sems, index, src, dst, where):
+        copy = copy_to(sems, index, src, dst, where)
+        copy.start()
+        pending.append(copy)
+
+    def arrive(sems, index, dst):
+        copy_to(sems, index, dst, dst, {"ts": me}).wait_recv()
+
+    sib_sems, x_sems, y_sems = (sib_send, sib_recv), (x_send, x_recv), (y_send, y_recv)
+    z_sems = (z_send, z_recv)
+    right, left = {"ts": node(0, 1)}, {"ts": node(0, -1)}
+    up, down = {"ts": node(1, 0)}, {"ts": node(-1, 0)}
+    ahead, behind = {"dp": chip(1)}, {"dp": chip(-1)}
+    sibling = {"dp": x * 2 + 1 - core}
+    zh = nz // 2
+
+    def y_part(dy, which):
+        return term_ref.at[pl.ds(which * zh, zh), lax.rem(y + dy + NY, NY)]
+
+    def y_half(buffer, way, which):
+        return buffer.at[way, pl.ds(which * zh, zh)]
+
+    send(y_sems, 0, y_part(2, 0), y_first.at[0], right)
+    send(y_sems, 1, y_part(2, 1), y_first.at[1], left)
+    send(y_sems, 2, y_part(1, 1), y_half(y_last, 0, 1), right)
+    send(y_sems, 3, y_part(-1, 0), y_half(y_last, 1, 0), left)
+
+    def lhs(ref, chip_at, m):
+        return ref[:, pl.ds(pl.multiple_of(chip_at * (2 * rows) + m * 128, 128), 128)]
+
+    order = (2, 1, -1, 0)
+    for j in range(4):
+        chip_at = lax.rem(x + order[j] + nx, nx)
+
+        @pl.loop(0, 2 * rows // 128)
+        def _(m):
+            at = pl.ds(pl.multiple_of(m * 128, 128), 128)
+            turned = (((0,), (0,)), ((), ()))
+            both = lax.dot_general(
+                lhs(normed_ref, chip_at, m), acts_ref[:, : 2 * hidden], turned, preferred_element_type=jnp.float32)
+            pair[j, at, : 2 * hidden] = (factor * both).astype(jnp.bfloat16)
+            one = lax.dot_general(
+                lhs(scaled_ref, chip_at, m), acts_ref[:, 2 * hidden :], turned, preferred_element_type=jnp.float32)
+            pair[j, at, 2 * hidden :] = (factor * one).astype(jnp.bfloat16)
+
+        for q in range(4):
+            theirs = pl.ds(pl.multiple_of((1 - core) * rows + q * quarter, 16), quarter)
+            send(sib_sems, 4 * j + q, pair.at[j, theirs], sib.at[j, pl.ds(q * quarter, quarter)], sibling)
+
+    def add(j, q, others, target):
+        arrive(sib_sems, 4 * j + q, sib.at[j, pl.ds(q * quarter, quarter)])
+
+        @pl.loop(0, quarter // 16)
+        def _(i):
+            mine = pl.ds(pl.multiple_of(core * rows + q * quarter + i * 16, 16), 16)
+            here = pl.ds(pl.multiple_of(q * quarter + i * 16, 16), 16)
+            total = pair[j, mine, :].astype(jnp.float32) + sib[j, here, :].astype(jnp.float32)
+            for ref, start in others:
+                total += ref[pl.ds(pl.multiple_of(start + i * 16, 16), 16), :].astype(jnp.float32)
+            target[pl.ds(pl.multiple_of(q * quarter + i * 16, 16), 16), :] = total.astype(jnp.bfloat16)
+
+    def chunk(ref, q):
+        return ref.at[pl.ds(q * quarter, quarter)]
+
+    for q in range(4):
+        add(0, q, (), sib.at[0])
+        way = q // 2
+        send(x_sems, q, chunk(sib.at[0], q), x_first.at[way, pl.ds((q % 2) * quarter, quarter)], (ahead, behind)[way])
+    for q in range(2):
+        add(1, 2 + q, (), sib.at[1])
+        send(x_sems, 4 + q, chunk(sib.at[1], 2 + q), chunk(x_last.at[0], 2 + q), ahead)
+        add(2, q, (), sib.at[2])
+        send(x_sems, 6 + q, chunk(sib.at[2], q), chunk(x_last.at[1], q), behind)
+
+    for way, dy, to in ((0, 1, right), (1, -1, left)):
+        arrive(y_sems, way, y_first.at[way])
+        for k in range(zh):
+            own = term_ref[way * zh + k, lax.rem(y + dy + NY, NY)].astype(jnp.float32)
+            y_first[way, k] = (own + y_first[way, k].astype(jnp.float32)).astype(jnp.bfloat16)
+        send(y_sems, 4 + way, y_first.at[way], y_half(y_last, way, way), to)
+    for way in range(2):
+        arrive(y_sems, 2 + way, y_half(y_last, way, 1 - way))
+        arrive(y_sems, 4 + way, y_half(y_last, way, way))
+
+    @pl.loop(0, nz)
+    def _(i):
+        at = lax.rem(z + i, nz)
+        total = term_ref[at, y].astype(jnp.float32) + y_last[0, at].astype(jnp.float32)
+        y_sum[i] = (total + y_last[1, at].astype(jnp.float32)).astype(jnp.bfloat16)
+
+    width = y_sum.shape[2]
+    cut = width // 256 * 128
+    halves = (pl.ds(0, cut), pl.ds(cut, width - cut))
+    send(z_sems, 0, y_sum.at[4, :, halves[0]], z_in.at[0, 0, :, halves[0]], up)
+    send(z_sems, 1, y_sum.at[4, :, halves[1]], z_in.at[1, 0, :, halves[1]], down)
+
+    for q in range(2):
+        arrive(x_sems, q, x_first.at[0, pl.ds(q * quarter, quarter)])
+        add(1, q, ((x_first.at[0], q * quarter),), sib.at[1])
+        send(x_sems, 8 + q, chunk(sib.at[1], q), chunk(x_last.at[0], q), ahead)
+        arrive(x_sems, 2 + q, x_first.at[1, pl.ds(q * quarter, quarter)])
+        add(2, 2 + q, ((x_first.at[1], q * quarter),), sib.at[2])
+        send(x_sems, 10 + q, chunk(sib.at[2], 2 + q), chunk(x_last.at[1], 2 + q), behind)
+
+    for s in range(1, 4):
+        for way, to in ((0, up), (1, down)):
+            own = y_sum[4 - s if way == 0 else 4 + s].astype(jnp.float32)
+            if s == 1:
+                arrive(z_sems, way, z_in.at[way, 0, :, halves[way]])
+                z_out[way, s] = own.astype(jnp.bfloat16)
+                landed = z_in[way, 0, :, halves[way]].astype(jnp.float32)
+                z_out[way, s, :, halves[way]] = (
+                    y_sum[4 - s if way == 0 else 4 + s, :, halves[way]].astype(jnp.float32) + landed
+                ).astype(jnp.bfloat16)
+            else:
+                arrive(z_sems, 2 * (s - 1) + way, z_in.at[way, s - 1])
+                z_out[way, s] = (own + z_in[way, s - 1].astype(jnp.float32)).astype(jnp.bfloat16)
+            send(z_sems, 2 * s + way, z_out.at[way, s], z_in.at[way, s], to)
+    for way in range(2):
+        arrive(z_sems, 6 + way, z_in.at[way, 3])
+
+    for t in range(width // 128):
+        at = pl.ds(t * 128, 128)
+        total = y_sum[0, :, at].astype(jnp.float32) + z_in[0, 3, :, at].astype(jnp.float32)
+        spread[:, t, :] = total + z_in[1, 3, :, at].astype(jnp.float32)
+    for k in range(rows_out.shape[0]):
+        rows_out[k] = spread[k].astype(jnp.bfloat16)
+
+    @pl.loop(0, n_ts)
+    def _(h):
+        slots_out[h] = rows_out[pick_ref[0, h]]
+
+    def back_copy(step):
+        to = lax.rem(me + step, n_ts)
+        return pltpu.make_async_remote_copy(
+            slots_out.at[to], back_ref.at[me], b_send.at[step], b_recv.at[step],
+            device_id={"ts": to}, device_id_type=MESH)
+
+    @pl.loop(1, n_ts)
+    def _(step):
+        back_copy(step).start()
+
+    back_ref[me] = slots_out[me]
+
+    for q in range(4):
+        for way in range(2):
+            index = (8 + q, 6 + q)[way] if q < 2 else (2 + q, 8 + q)[way]
+            arrive(x_sems, index, chunk(x_last.at[way], q))
+        add(3, q, ((x_last.at[0], q * quarter), (x_last.at[1], q * quarter)), out_ref)
+
+    @pl.loop(1, n_ts)
+    def _(step):
+        back_copy(step).wait_send()
+        source = lax.rem(me - step + n_ts, n_ts)
+        pltpu.make_async_remote_copy(
+            slots_out.at[source], back_ref.at[source], b_send.at[step], b_recv.at[step],
+            device_id={"ts": source}, device_id_type=MESH).wait_recv()
+
+    for copy in pending:
+        copy.wait_send()
+
+
+def reduce_all(pick, normed, scaled, acts, term, n_ts, n_dp, factor):
+    nz = n_ts // NY
+    rows = normed.shape[1] // n_dp
+    wide = acts.shape[1]
+    piece = term.shape[2:]
+    tiles = piece[1] // 128
+    pad = -(-tiles // 16) * 16
+    bf16, dma = jnp.bfloat16, pltpu.SemaphoreType.DMA
+    vmem = pl.BlockSpec(memory_space=pltpu.VMEM)
+    return pl.pallas_call(
+        functools.partial(reduce_kernel, n_ts, n_dp, factor),
+        out_shape=(
+            jax.ShapeDtypeStruct((rows, wide), bf16),
+            jax.ShapeDtypeStruct((n_ts, pad, 128), bf16),
+        ),
+        in_specs=[pl.BlockSpec(memory_space=pltpu.SMEM)] + [vmem] * 4,
+        out_specs=(vmem, vmem),
+        scratch_shapes=[
+            pltpu.VMEM((4, 2 * rows, wide), bf16),
+            pltpu.VMEM((4, rows, wide), bf16),
+            pltpu.VMEM((2, rows // 2, wide), bf16),
+            pltpu.VMEM((2, rows, wide), bf16),
+            pltpu.VMEM((2, nz // 2) + piece, bf16),
+            pltpu.VMEM((2, nz) + piece, bf16),
+            pltpu.VMEM((nz,) + piece, bf16),
+            pltpu.VMEM((2, 4) + piece, bf16),
+            pltpu.VMEM((2, 4) + piece, bf16),
+            pltpu.VMEM((piece[0], pad, 128), jnp.float32),
+            pltpu.VMEM((piece[0], pad, 128), bf16),
+            pltpu.VMEM((n_ts, pad, 128), bf16),
+            dma((16,)), dma((16,)), dma((12,)), dma((12,)), dma((6,)), dma((6,)),
+            dma((8,)), dma((8,)), dma((n_ts,)), dma((n_ts,)),
+        ],
+        compiler_params=pltpu.CompilerParams(
+            collective_id=1, has_side_effects=True, vmem_limit_bytes=44 * 1024 * 1024),
+        name="reduce_all",
+    )(pick, normed, scaled, acts, term)
 
 
 epsilon = 1e-06
@@ -265,19 +499,15 @@
     normed_term = normed_term + jnp.einsum("cf,df->cd", up_in, expand_matrix, preferred_element_type=jnp.float32)
     term = jnp.concatenate(
         [normed_term, jnp.broadcast_to(dot_part[:, None], (cap, 128))], axis=1).astype(jnp.bfloat16)
-    own_sum = lax.psum_scatter(term, "ts", scatter_dimension=0, tiled=True)
-    gate_term = jnp.einsum("cd,cf->df", normed, gate_in, preferred_element_type=jnp.float32)
-    up_term = jnp.einsum("cd,cf->df", normed, up_in, preferred_element_type=jnp.float32)
-    down_term = jnp.einsum("cd,cf->df", scaled, hidden, preferred_element_type=jnp.float32)
-    parts = (factor * jnp.concatenate([gate_term, up_term, down_term], axis=1)).astype(jnp.bfloat16)
-    summed_weights = reduce_weights(parts)
+    acts = jnp.concatenate([gate_in, up_in, hidden], axis=1)
+    class_holder = jnp.take(kept.reshape(-1, n_ts), me, axis=1) // local_tokens
+    pick = jnp.argmax(class_holder[None, :] == classes[:, None], axis=1).astype(jnp.int32)[None]
+    summed_weights, back = reduce_all(
+        pick, normed, scaled, acts, term.reshape(n_ts // NY, NY, cap // n_ts, -1), n_ts, n_dp, factor)
     gate_grad = summed_weights[:, :hidden_width]
     up_grad = summed_weights[:, hidden_width : 2 * hidden_width]
     down_grad = summed_weights[:, 2 * hidden_width :].T
-
-    class_holder = jnp.take(kept.reshape(-1, n_ts), me, axis=1) // local_tokens
-    pick = jnp.argmax(class_holder[None, :] == classes[:, None], axis=1)
-    back = lax.all_to_all(jnp.take(own_sum, pick, axis=0), "ts", split_axis=0, concat_axis=0, tiled=True)
+    back = back.reshape(n_ts, -1)
     own_term = back[:, :model_width].astype(jnp.float32)
     own_dot = back[:, model_width].astype(jnp.float32)
     row_grad = norm_backward(own_rows, own_term, own_dot, prenormal_scaling, scorer_matrix)

time: 285 us -> 179 us (0.63)
  waiting for transfers between devices: 133 us -> 0 us
  Pallas kernels: 57.9 us -> 114 us
  between operations: 20.2 us -> 4.18 us
  local copies, waits for them, and re-layouts: 35.5 us -> 28.6 us
  starting transfers between devices: 5.61 us -> 0 us
    unnamed x4 -> x0, waiting for transfers between devices: 124 us -> none
    pallas_call x0 -> x1, Pallas kernels: none -> 56.3 us  [reduce_all(): pl.pallas_call(functools.partial(reduce_kernel, n_ts, n_dp, factor), out_...]
    unnamed x41 -> x40, local copies, waits for them, and re-layouts: 25.2 us -> 13.5 us
    all_to_all x1 -> x0, waiting for transfers between devices: 9.06 us -> none  [local(): lax.all_to_all(jnp.take(own_sum, pick, axis=0), 'ts', split_axis=0, conca...]
    all_to_all x1 -> x0, starting transfers between devices: 5.34 us -> none  [local(): lax.all_to_all(jnp.take(own_sum, pick, axis=0), 'ts', split_axis=0, conca...]
    dot_general x3 -> x0, matrix products: 5.01 us -> none  [the longest x1 2.78 us: local(): jnp.einsum('cd,cf->df', normed, up_in, preferred_element_type=jnp.float32)]
    dot_general x0 -> x2, local copies, waits for them, and re-layouts: none -> 4.04 us  [the longest x1 2.03 us: local(): pre_up = jnp.dot(normed, expand_matrix, preferred_element_type=jnp.float32)]
    convert_element_type x1, other arithmetic: 6.86 us -> 3.29 us  [local(): (weight[:, None] * grad_data.astype(jnp.float32)).astype(jnp.bfloat16)]
  transfers between devices with their start and end apart: 3 -> 0, of which waited for: 2 -> 0; matrix products, arithmetic and copies ran while one was open for 13% -> 0% of each run, Pallas kernels for 0% -> 0%
where the time goes in v2:
time: 179 us; the launch traced here: 177 us
  Pallas kernels  114 us (64%)
  local copies, waits for them, and re-layouts  28.6 us (16%)
  matrix products  15.8 us (9%)
  other arithmetic  14.2 us (8%)
  between operations  4.18 us (2%)
    pallas_call x1, Pallas kernels, gather_rows(): pl.pallas_call(functools.partial(gather_kernel, n_ts, block), out_shape=j...  57.9 us
    pallas_call x1, Pallas kernels, reduce_all(): pl.pallas_call(functools.partial(reduce_kernel, n_ts, n_dp, factor), out_...  56.3 us
    unnamed x40, local copies, waits for them, and re-layouts  13.5 us
    dot_general x1, matrix products, local(): jnp.dot(normed, switch_matrix, preferred_element_type=jnp.float32)  4.1 us

profile of v2, /device:TPU:2, one launch (start us, length us, event | category | flops | bytes accessed | tf_op | source)
XLA Modules:
  0.0 177.0 jit_solution(11880273705585347727)
XLA Ops:
  0.6 1.5 fusion.42
  4.8 1.4 gather_fusion
  8.2 2.0 %gather_fusion.2 = bf16[32,3584]{1,0:T(8,128)(2,1)S(1)} fusion(bf16[64,3584]{1,0:T(8,128)(2,1)} %bitcast.62, s32[1024]{0:T(1024)S(1)} %pad_clamp_fusion), kind=kCustom, calls=%fused_computation.1.clone | custom fusion | bytes 458880 | tf_op jit(solution)/shard_map/jit(_take)/gather | solution.py:479
  10.1 0.8 broadcast_select_fusion
  10.9 2.0 %gather_fusion.1 = bf16[32,3584]{1,0:T(8,128)(2,1)S(1)} fusion(bf16[64,3584]{1,0:T(8,128)(2,1)} %bitcast.63, s32[1024]{0:T(1024)S(1)} %pad_clamp_fusion), kind=kCustom, calls=%fused_computation.clone | custom fusion | bytes 458880 | tf_op jit(solution)/shard_map/jit(_take)/gather | solution.py:478
  13.2 1.1 maximum_bitcast_fusion
  14.3 57.9 %gather_rows.1 = bf16[2,32,8,3584]{3,2,1,0:T(8,128)(2,1)S(1)} custom-call(s32[1,256]{1,0:T(1,128)S(1)} %copy-done.1, bf16[32,56,128]{2,1,0:T(8,128)(2,1)S(1)} %bitcast.59), custom_call_target="tpu_custom_call" | custom-call | tf_op jit(solution)/shard_map/gather_rows/pallas_call | solution.py:177
  72.3 1.8 %copy-done.2 = bf16[2,32,8,3584]{3,2,1,0:T(8,128)(2,1)} copy-done((bf16[2,32,8,3584]{3,2,1,0:T(8,128)(2,1)}, bf16[2,32,8,3584]{3,2,1,0:T(8,128)(2,1)S(1)}, u32[]{:S(2)}) %copy-start.2) | copy-done | bytes 3670040
  74.6 2.1 %fusion.3 = f32[1,256]{1,0:T(1,128)S(1)} fusion(bf16[3584,1]{0,1:T(2,128)(2,1)S(1)} %reshape.233, bf16[2,32,8,3584]{3,2,1,0:T(8,128)(2,1)} %copy-done.2), kind=kOutput, calls=%fused_computation.12 | convolution fusion | flops 1835008 | bytes 1843200 | tf_op jit(solution)/shard_map/dot_general | solution.py:488
  76.7 3.3 %fusion.2 = (bf16[256,3584]{1,0:T(8,128)(2,1)S(1)}, bf16[256,3584]{1,0:T(8,128)(2,1)S(1)}) fusion(bf16[2,32,8,3584]{3,2,1,0:T(8,128)(2,1)} %copy-done.2, f32[256]{0:T(256)S(1)} %add_divide_fusion, f32[3584]{0:T(1024)S(1)} %convert_element_type.69, f32[256]{0:T(256)S(1)} %rsqrt.21), kind=kLoop, calls=%fused_computation.8 | loop fusion | flops 6422528 | bytes 7356416 | tf_op jit(solution)/shard_map/convert_element_type | solution.py:493
  80.1 1.0 fusion.52
  81.1 2.3 %copy-done.9 = bf16[448,3584]{1,0:T(8,128)(2,1)S(1)} copy-done((bf16[448,3584]{1,0:T(8,128)(2,1)S(1)}, bf16[448,3584]{1,0:T(8,128)(2,1)}, u32[]{:S(2)}) %copy-start.9) | copy-done | bytes 3211288
  83.5 1.9 %fusion.51 = (f32[256,448]{0,1:T(8,128)}, f32[256,448]{0,1:T(8,128)}) fusion(f32[256,448]{0,1:T(8,128)S(1)} %fusion.52, bf16[256,3584]{1,0:T(8,128)(2,1)S(1)} %get-tuple-element.46.scaled_ref, bf16[448,3584]{1,0:T(8,128)(2,1)S(1)} %copy-done.9), kind=kOutput, calls=%fused_computation.106 | convolution fusion | flops 822198272 | bytes 6422528 | tf_op jit(solution)/shard_map/cd,fd->cf/dot_general | solution.py:494
  85.4 2.0 %copy.62 = f32[256,448]{1,0:T(8,128)} copy(f32[256,448]{0,1:T(8,128)} %get-tuple-element.53) | data formatting | bytes 917504 | tf_op jit(solution)/shard_map/mul | solution.py:495
  87.5 2.0 %copy.63 = f32[256,448]{1,0:T(8,128)} copy(f32[256,448]{0,1:T(8,128)} %get-tuple-element.54) | data formatting | bytes 917504 | tf_op jit(solution)/shard_map/cd,fd->cf/dot_general | solution.py:494
  89.5 2.0 %copy.64 = f32[256,448]{1,0:T(8,128)} copy(f32[256,448]{0,1:T(8,128)} %copy-done.13) | data formatting | bytes 917504 | tf_op jit(solution)/shard_map/dot_general | solution.py:490
  91.5 4.1 %multiply_reduce_fusion.1 = (bf16[256]{0:T(256)(128)(2,1)S(1)}, bf16[256,448]{1,0:T(8,128)(2,1)}, bf16[256,448]{1,0:T(8,128)(2,1)S(1)}, bf16[256,448]{1,0:T(8,128)(2,1)S(1)}) fusion(f32[256,448]{1,0:T(8,128)} %copy.63, f32[256,448]{1,0:T(8,128)} %copy.64, f32[256,448]{1,0:T(8,128)} %copy.62, bf16[256,3584]{1,0:T(8,128)(2,1)} %copy-done.6, ...), kind=kOutput, calls=%fused_computation.35 | convolution fusion | flops 825179904 | bytes 7111168 | tf_op jit(solution)/shard_map/dot_general | solution.py:489
  95.6 1.1 fusion.53
  96.7 0.9 copy-done.11
  97.6 2.4 %fusion = bf16[256,3584]{1,0:T(8,128)(2,1)} fusion(f32[256,3584]{1,0:T(8,128)S(1)} %fusion.53, bf16[256,448]{1,0:T(8,128)(2,1)S(1)} %get-tuple-element.51, bf16[3584,448]{0,1:T(8,128)(2,1)S(1)} %copy-done.11), kind=kOutput, calls=%fused_computation.4 | convolution fusion | flops 823918592 | bytes 8945664 | tf_op jit(solution)/shard_map/cf,df->cd/dot_general | solution.py:499
  100.2 2.9 %pad_maximum_fusion.term_ref = bf16[8,4,8,3712]{3,2,1,0:T(8,128)(2,1)} fusion(bf16[8,4,8,128]{3,2,1,0:T(8,128)(2,1)S(1)} %broadcast_in_dim.69, bf16[8,4,8,3584]{3,2,1,0:T(8,128)(2,1)} %bitcast.64), kind=kLoop, calls=%fused_computation.11 | loop fusion | flops 3801088 | bytes 3801088 | tf_op jit(solution)/shard_map/concatenate | solution.py:500
  103.1 2.0 %concatenate.14.acts_ref = bf16[256,1344]{1,0:T(8,128)(2,1)} concatenate(bf16[256,448]{1,0:T(8,128)(2,1)S(1)} %get-tuple-element.52, bf16[256,448]{1,0:T(8,128)(2,1)} %copy-done.14, bf16[256,448]{1,0:T(8,128)(2,1)} %get-tuple-element.43), dimensions={1} | concatenate | bytes 1376256 | tf_op jit(solution)/shard_map/concatenate | solution.py:502
  107.2 1.5 copy-done.4
  108.7 1.5 copy-done.5
  110.2 1.5 copy-done.7
  111.7 1.1 copy-done.8
  112.8 56.3 %reduce_all.1 = (bf16[448,1344]{1,0:T(8,128)(2,1)S(1)}, bf16[32,32,128]{2,1,0:T(8,128)(2,1)S(1)}) custom-call(s32[1,32]{1,0:T(1,128)S(1)} %bitcast.61, bf16[256,3584]{1,0:T(8,128)(2,1)S(1)} %copy-done.7, bf16[256,3584]{1,0:T(8,128)(2,1)S(1)} %copy-done.4, bf16[256,1344]{1,0:T(8,128)(2,1)S(1)} %copy-done.8, bf16[8,4,8,3712]{3,2,1,0:T(8,128)(2,1)S(1)} %copy-done.5), custom_call_target="tpu_custom_call" | custom-call | tf_op jit(solution)/shard_map/reduce_all/pallas_call | solution.py:404
  169.1 1.3 slice_bitcast_fusion
  170.4 2.0 %copy.66 = bf16[448,448]{1,0:T(8,128)(2,1)} copy(bf16[448,448]{0,1:T(8,128)(2,1)} %get-tuple-element.48) | data formatting | bytes 802816
  172.5 1.2 fusion.21
  173.8 1.1 fusion.11
  174.9 2.1 %fusion.1 = bf16[1,64,3584]{2,1,0:T(8,128)(2,1)} fusion(bf16[32,3584]{1,0:T(8,128)(2,1)} %copy-done.12, f32[3584]{0:T(1024)S(1)} %convert_element_type.81, f32[32]{0:T(128)S(1)} %fusion.11, f32[32]{0:T(128)S(1)} %broadcast_multiply_fusion, f32[3584]{0:T(1024)S(1)} %convert_element_type.69, f32[32]{0:T(128)S(1)} %add_rsqrt_fusion.1, ...), kind=kOutput, calls=%fused_computation.6 | convolution fusion | flops 16175104 | bytes 953344 | tf_op jit(solution)/shard_map/dot_general | solution.py:516
  (54 shorter events, 4.8 us)
Async XLA Ops:
  0.6 90.9 %copy-start = (bf16[3584,448]{0,1:T(8,128)(2,1)S(1)}, bf16[3584,448]{0,1:T(8,128)(2,1)}, u32[]{:S(2)}) copy-start(bf16[3584,448]{0,1:T(8,128)(2,1)} %param.15) | copy-start | bytes 9633796
  8.1 6.2 %copy-start.1 = (s32[1,256]{1,0:T(1,128)S(1)}, s32[1,256]{1,0:T(1,128)}, u32[]{:S(2)}) copy-start(s32[1,256]{1,0:T(1,128)} %kept_ref.1) | copy-start | bytes 3076
  13.2 1.1 copy-start.12
  14.3 60.3 %copy-start.15 = (bf16[3584]{0:T(1024)(128)(2,1)S(1)}, bf16[3584]{0:T(1024)(128)(2,1)}, u32[]{:S(2)}) copy-start(bf16[3584]{0:T(1024)(128)(2,1)} %param.14) | copy-start | bytes 21508
  14.3 62.4 %copy-start.16 = (bf16[3584]{0:T(1024)(128)(2,1)S(1)}, bf16[3584]{0:T(1024)(128)(2,1)}, u32[]{:S(2)}) copy-start(bf16[3584]{0:T(1024)(128)(2,1)} %param.13) | copy-start | bytes 21508
  72.2 1.8 %copy-start.2 = (bf16[2,32,8,3584]{3,2,1,0:T(8,128)(2,1)}, bf16[2,32,8,3584]{3,2,1,0:T(8,128)(2,1)S(1)}, u32[]{:S(2)}) copy-start(bf16[2,32,8,3584]{3,2,1,0:T(8,128)(2,1)S(1)} %gather_rows.1) | copy-start | bytes 11010052
  76.7 3.3 %copy-start.10 = (bf16[3584,448]{0,1:T(8,128)(2,1)S(1)}, bf16[3584,448]{0,1:T(8,128)(2,1)}, u32[]{:S(2)}) copy-start(bf16[3584,448]{0,1:T(8,128)(2,1)} %param.16) | copy-start | bytes 9633796
  80.0 5.4 %copy-start.3 = (bf16[256,3584]{1,0:T(8,128)(2,1)}, bf16[256,3584]{1,0:T(8,128)(2,1)S(1)}, u32[]{:S(2)}) copy-start(bf16[256,3584]{1,0:T(8,128)(2,1)S(1)} %get-tuple-element.46.scaled_ref) | copy-start | bytes 5505028
  80.0 5.4 %copy-start.6 = (bf16[256,3584]{1,0:T(8,128)(2,1)}, bf16[256,3584]{1,0:T(8,128)(2,1)S(1)}, u32[]{:S(2)}) copy-start(bf16[256,3584]{1,0:T(8,128)(2,1)S(1)} %get-tuple-element.47.normed_ref) | copy-start | bytes 5505028
  80.1 3.4 %copy-start.9 = (bf16[448,3584]{1,0:T(8,128)(2,1)S(1)}, bf16[448,3584]{1,0:T(8,128)(2,1)}, u32[]{:S(2)}) copy-start(bf16[448,3584]{1,0:T(8,128)(2,1)} %param.17) | copy-start | bytes 9633796
  81.1 4.3 %copy-start.13 = (f32[256,448]{0,1:T(8,128)}, f32[256,448]{0,1:T(8,128)S(1)}, u32[]{:S(2)}) copy-start(f32[256,448]{0,1:T(8,128)S(1)} %fusion.52) | copy-start | bytes 1376260
  95.6 1.1 copy-start.14
  95.6 2.0 %copy-start.11 = (bf16[3584,448]{0,1:T(8,128)(2,1)S(1)}, bf16[3584,448]{0,1:T(8,128)(2,1)}, u32[]{:S(2)}) copy-start(bf16[3584,448]{0,1:T(8,128)(2,1)} %param.16) | copy-start | bytes 9633796
  107.2 1.5 copy-start.4
  108.7 1.5 copy-start.5
  110.2 1.5 copy-start.7
  111.7 1.1 copy-start.8

commit v3 on v0

v3 whole, which is shorter than its diff:
```python
import functools
import math

import jax
import jax.numpy as jnp
from jax import lax
from jax.experimental import pallas as pl
from jax.experimental.pallas import tpu as pltpu
from jax.sharding import PartitionSpec as P

MESH = pl.DeviceIdType.MESH
NY = 4
Z_STEPS = (0, -1, 1, -2, 2, -3, 3, 4)
LANES = 128
K_TILE = 512
epsilon = 1e-06
gelu_scale = math.sqrt(2.0 / math.pi)
ROWS_BY_ROWS = (((0,), (0,)), ((), ()))
COLS_BY_COLS = (((1,), (1,)), ((), ()))


def gelu_pair(pre_act):
    cubic = pre_act + 0.044715 * pre_act * pre_act * pre_act
    tanh_part = jnp.tanh(gelu_scale * cubic)
    gelu_out = 0.5 * pre_act * (1.0 + tanh_part)
    slope_out = 0.5 * (1.0 + tanh_part) + 0.5 * pre_act * (
        1.0 - tanh_part * tanh_part
    ) * gelu_scale * (1.0 + 3.0 * 0.044715 * pre_act * pre_act)
    return (gelu_out, slope_out)


def dot(a, b, dims=(((1,), (0,)), ((), ()))):
    return lax.dot_general(a, b, dims, preferred_element_type=jnp.float32)


def block_kernel(
    n_ts, n_dp, factor,
    kept_ref, kept_row, act_ref, cot_ref, gain_ref, scorer_ref, switch_hbm, expand_hbm, contract_hbm,
    token_ref, gate_ref, up_ref, down_ref,
    switch, expand, contract, w_sem,
    own, slots_f, slots, landed, wide, piece_f, full, p1_send, p1_recv, g_send, g_recv,
    pre_gate, pre_up, hidden_grad, gate_in, up_in, acts, hidden, term,
    pair, sib, x_first, x_last, y_first, y_last, y_sum, z_in, z_out, spread, rows_out, slots_out, back, back_f, term_f,
    sib_send, sib_recv, x_send, x_recv, y_send, y_recv, z_send, z_recv, b_send, b_recv,
):
    bf16, f32 = jnp.bfloat16, jnp.float32
    nz = n_ts // NY
    nx = n_dp // 2
    me = lax.axis_index("ts")
    z, y = me // NY, lax.rem(me, NY)
    dp = lax.axis_index("dp")
    x, core = dp // 2, lax.rem(dp, 2)
    block, width = act_ref.shape
    tiles = width // LANES
    piece_rows = full.shape[2]
    cap = n_ts * piece_rows
    hid = hidden.shape[1]
    pending = []

    def node(dz, dy):
        return lax.rem(z + dz + nz, nz) * NY + lax.rem(y + dy + NY, NY)

    def chip(dx):
        return lax.rem(x + dx + nx, nx) * 2 + core

    def copy_to(sems, index, src, dst, where):
        return pltpu.make_async_remote_copy(
            src, dst, sems[0].at[index], sems[1].at[index], device_id=where, device_id_type=MESH)

    def send(sems, index, src, dst, where):
        copy = copy_to(sems, index, src, dst, where)
        copy.start()
        pending.append(copy)

    def arrive(sems, index, dst):
        copy_to(sems, index, dst, dst, {"ts": me}).wait_recv()

    right, left = {"ts": node(0, 1)}, {"ts": node(0, -1)}
    up, down = {"ts": node(1, 0)}, {"ts": node(-1, 0)}
    ahead, behind = {"dp": chip(1)}, {"dp": chip(-1)}
    sibling = {"dp": x * 2 + 1 - core}

    barrier = pltpu.get_barrier_semaphore()

    @pl.loop(1, n_ts)
    def _(step):
        pl.semaphore_signal(barrier, inc=1, device_id={"ts": lax.rem(me + step, n_ts)}, device_id_type=MESH)

    for where in (sibling, ahead, behind):
        pl.semaphore_signal(barrier, inc=1, device_id=where, device_id_type=MESH)

    weight_copies = [
        pltpu.make_async_copy(src, dst, w_sem.at[i])
        for i, (src, dst) in enumerate(((switch_hbm, switch), (expand_hbm, expand), (contract_hbm, contract)))
    ]
    for copy in weight_copies:
        copy.start()

    kept = jnp.broadcast_to(kept_row[...], (block, cap))
    position = lax.broadcasted_iota(jnp.int32, (block, cap), 0) + block * me
    rank = jnp.sum((kept < position).astype(f32), axis=1, keepdims=True)
    routed = jnp.sum((kept == position).astype(f32), axis=1, keepdims=True)
    row_class = rank - n_ts * jnp.floor(rank * (1.0 / n_ts))
    classes = lax.broadcasted_iota(jnp.int32, (block, n_ts), 1).astype(f32)
    chosen = jnp.where(classes == row_class, routed, 0.0).astype(bf16)
    own[...] = dot(chosen, act_ref[...], ROWS_BY_ROWS)
    own_cot = dot(chosen, cot_ref[...], ROWS_BY_ROWS)
    for t in range(tiles):
        slots_f[:, t, :] = own[:, t * LANES:(t + 1) * LANES]
        slots_f[:, tiles + t, :] = own_cot[:, t * LANES:(t + 1) * LANES]

    @pl.loop(0, n_ts)
    def _(c):
        slots[c] = slots_f[c].astype(bf16)

    pl.semaphore_wait(barrier, n_ts - 1 + 3)

    def p1_copy(step):
        to = lax.rem(me + step, n_ts)
        return pltpu.make_async_remote_copy(
            slots.at[to], landed.at[me], p1_send.at[step], p1_recv.at[step],
            device_id={"ts": to}, device_id_type=MESH)

    @pl.loop(1, n_ts)
    def _(step):
        p1_copy(step).start()

    landed[me] = slots[me]

    @pl.loop(1, n_ts)
    def _(step):
        source = lax.rem(me - step + n_ts, n_ts)
        pltpu.make_async_remote_copy(
            slots.at[source], landed.at[source], p1_send.at[step], p1_recv.at[step],
            device_id={"ts": source}, device_id_type=MESH).wait_recv()

    for k in range(piece_rows):
        wide[k] = landed[kept_ref[0, n_ts * k + me] // block].astype(f32)
    for t in range(2 * tiles):
        piece_f[:, t * LANES:(t + 1) * LANES] = wide[:, t, :]

    gain = gain_ref[...].astype(f32)
    scorer = scorer_ref[...].astype(f32)
    row_f = piece_f[:, :width]
    inv_rms = lax.rsqrt(jnp.sum(row_f * row_f, axis=1, keepdims=True) * (1.0 / width) + epsilon)
    weight = jax.nn.sigmoid(jnp.sum(row_f * scorer, axis=1, keepdims=True))
    full[0, me] = (row_f * inv_rms * gain).astype(bf16)
    full[1, me] = (weight * piece_f[:, width:]).astype(bf16)

    g_sems = (g_send, g_recv)
    half = width // 2

    def piece(part, n):
        return full.at[part, n]

    def piece_half(part, n, which):
        return full.at[part, n, :, pl.ds(which * half, half)]

    def group(dz):
        return full.at[1, pl.ds(lax.rem(z + dz + nz, nz) * NY, NY)]

    def group_half(dz, which):
        return full.at[1, pl.ds(lax.rem(z + dz + nz, nz) * NY + which * (NY // 2), NY // 2)]

    def share(index, ref, where):
        send(g_sems, index, ref, ref, where)

    B1, A1, B2, A2, A3 = 0, 4, 12, 20, 36
    share(B1 + 0, piece(1, me), right)
    share(B1 + 1, piece(1, me), left)
    share(A1 + 0, piece(0, me), up)
    share(A1 + 1, piece(0, me), down)

    def fan_out(j):
        dz = Z_STEPS[j]
        share(A2 + 2 * j, piece(0, node(dz, 0)), right)
        share(A2 + 2 * j + 1, piece(0, node(dz, 0)), left)

    def relay(j):
        dz = Z_STEPS[j]
        arrive(g_sems, A2 + 2 * j, piece(0, node(dz, -1)))
        share(A3 + 2 * j, piece_half(0, node(dz, -1), 0), right)
        arrive(g_sems, A2 + 2 * j + 1, piece(0, node(dz, 1)))
        share(A3 + 2 * j + 1, piece_half(0, node(dz, 1), 1), left)

    def along(s):
        if s < 4:
            arrive(g_sems, A1 + 2 * (s - 1), piece(0, node(-s, 0)))
            if s < 3:
                share(A1 + 2 * s, piece(0, node(-s, 0)), up)
            else:
                share(A1 + 6, piece_half(0, node(-3, 0), 0), up)
            arrive(g_sems, A1 + 2 * (s - 1) + 1, piece(0, node(s, 0)))
            if s < 3:
                share(A1 + 2 * s + 1, piece(0, node(s, 0)), down)
            else:
                share(A1 + 7, piece_half(0, node(3, 0), 1), down)
            fan_out(2 * s - 1)
            fan_out(2 * s)
        else:
            arrive(g_sems, A1 + 6, piece_half(0, node(-4, 0), 0))
            arrive(g_sems, A1 + 7, piece_half(0, node(4, 0), 1))
            fan_out(7)

    def groups(s):
        if s < 4:
            arrive(g_sems, B2 + 2 * (s - 1), group(-s))
            if s < 3:
                share(B2 + 2 * s, group(-s), up)
            else:
                share(B2 + 6, group_half(-3, 0), up)
            arrive(g_sems, B2 + 2 * (s - 1) + 1, group(s))
            if s < 3:
                share(B2 + 2 * s + 1, group(s), down)
            else:
                share(B2 + 7, group_half(3, 1), down)
        else:
            arrive(g_sems, B2 + 6, group_half(-4, 0))
            arrive(g_sems, B2 + 7, group_half(4, 1))

    fan_out(0)
    arrive(g_sems, B1 + 0, piece(1, node(0, -1)))
    share(B1 + 2, piece_half(1, node(0, -1), 0), right)
    arrive(g_sems, B1 + 1, piece(1, node(0, 1)))
    share(B1 + 3, piece_half(1, node(0, 1), 1), left)
    along(1)
    arrive(g_sems, B1 + 2, piece_half(1, node(0, -2), 0))
    arrive(g_sems, B1 + 3, piece_half(1, node(0, 2), 1))
    share(B2 + 0, group(0), up)
    share(B2 + 1, group(0), down)
    along(2)
    relay(0)
    along(3)
    relay(1)
    relay(2)
    groups(1)
    along(4)
    relay(3)
    relay(4)
    groups(2)
    relay(5)
    relay(6)
    relay(7)
    groups(3)
    for j in range(8):
        arrive(g_sems, A3 + 2 * j, piece_half(0, node(Z_STEPS[j], -2), 0))
        arrive(g_sems, A3 + 2 * j + 1, piece_half(0, node(Z_STEPS[j], 2), 1))

    def columns(part, start, size):
        return full[part, :, :, pl.ds(pl.multiple_of(start, LANES), size)].reshape(cap, size)

    for copy in weight_copies:
        copy.wait()
    pre_gate[...] = jnp.zeros_like(pre_gate)
    pre_up[...] = jnp.zeros_like(pre_up)
    hidden_grad[...] = jnp.zeros_like(hidden_grad)

    @pl.loop(0, width // K_TILE)
    def _(k):
        at = pl.ds(pl.multiple_of(k * K_TILE, K_TILE), K_TILE)
        normed = columns(0, k * K_TILE, K_TILE)
        pre_gate[...] += dot(normed, switch[at, :])
        pre_up[...] += dot(normed, expand[at, :])

    groups(4)

    @pl.loop(0, width // K_TILE)
    def _(k):
        at = pl.ds(pl.multiple_of(k * K_TILE, K_TILE), K_TILE)
        hidden_grad[...] += dot(columns(1, k * K_TILE, K_TILE), contract[:, at], COLS_BY_COLS)

    @pl.loop(0, nz)
    def _(i):
        n = cap // nz
        at = pl.ds(pl.multiple_of(i * n, n), n)
        gelu_out, slope_out = gelu_pair(pre_gate[at, :])
        up_value, grad = pre_up[at, :], hidden_grad[at, :]
        hidden_value = (gelu_out * up_value).astype(bf16)
        hidden[at, :] = hidden_value
        gate_value = (grad * up_value * slope_out).astype(bf16)
        up_back = (grad * gelu_out).astype(bf16)
        gate_in[at, :] = gate_value
        up_in[at, :] = up_back
        acts[at, :hid] = gate_value
        acts[at, hid:] = up_back
        router = jnp.sum(hidden_value.astype(f32) * grad, axis=1, keepdims=True)
        term[i, :, :, width:] = jnp.broadcast_to(router, (n, LANES)).astype(bf16).reshape(NY, piece_rows, LANES)

    sib_sems, x_sems, y_sems = (sib_send, sib_recv), (x_send, x_recv), (y_send, y_recv)
    z_sems = (z_send, z_recv)
    rows = sib.shape[1]
    quarter = rows // 4
    order = (2, 1, -1, 0)

    def partials(j):
        start = lax.rem(x + order[j] + nx, nx) * (2 * rows)

        @pl.loop(0, 2 * rows // LANES)
        def _(m):
            at = pl.ds(pl.multiple_of(m * LANES, LANES), LANES)
            pair[j, at, : 2 * hid] = (
                factor * dot(columns(0, start + m * LANES, LANES), acts[...], ROWS_BY_ROWS)).astype(bf16)

        both = (factor * dot(hidden[...], columns(1, start, 2 * rows), ROWS_BY_ROWS)).astype(bf16)
        pair[j, :rows, 2 * hid :] = both[:, :rows]
        pair[j, rows:, 2 * hid :] = both[:, rows:]
        for q in range(4):
            theirs = pl.ds(pl.multiple_of((1 - core) * rows + q * quarter, 16), quarter)
            send(sib_sems, 4 * j + q, pair.at[j, theirs], sib.at[j, pl.ds(q * quarter, quarter)], sibling)

    def add(j, q, others, store):
        arrive(sib_sems, 4 * j + q, sib.at[j, pl.ds(q * quarter, quarter)])

        @pl.loop(0, quarter // 16)
        def _(i):
            mine = pl.ds(pl.multiple_of(core * rows + q * quarter + i * 16, 16), 16)
            here = pl.ds(pl.multiple_of(q * quarter + i * 16, 16), 16)
            total = pair[j, mine, :].astype(f32) + sib[j, here, :].astype(f32)
            for ref, start in others:
                total += ref[pl.ds(pl.multiple_of(start + i * 16, 16), 16), :].astype(f32)
            store(here, total.astype(bf16))

    def in_place(j):
        def store(here, value):
            sib[j, here, :] = value
        return store

    def chunk(ref, q):
        return ref.at[pl.ds(q * quarter, quarter)]

    partials(0)
    partials(1)
    for q in range(4):
        add(0, q, (), in_place(0))
        way = q // 2
        send(x_sems, q, chunk(sib.at[0], q), x_first.at[way, pl.ds((q % 2) * quarter, quarter)], (ahead, behind)[way])
    partials(2)

    @pl.loop(0, width // K_TILE)
    def _(k):
        at = pl.ds(pl.multiple_of(k * K_TILE, K_TILE), K_TILE)
        value = dot(gate_in[...], switch[at, :], COLS_BY_COLS) + dot(up_in[...], expand[at, :], COLS_BY_COLS)
        term[:, :, :, at] = value.astype(bf16).reshape(nz, NY, piece_rows, K_TILE)

    zh = nz // 2

    def y_part(dy, which):
        return term.at[pl.ds(which * zh, zh), lax.rem(y + dy + NY, NY)]

    def y_half(buffer, way, which):
        return buffer.at[way, pl.ds(which * zh, zh)]

    send(y_sems, 0, y_part(2, 0), y_first.at[0], right)
    send(y_sems, 1, y_part(2, 1), y_first.at[1], left)
    send(y_sems, 2, y_part(1, 1), y_half(y_last, 0, 1), right)
    send(y_sems, 3, y_part(-1, 0), y_half(y_last, 1, 0), left)

    for q in range(2):
        add(1, 2 + q, (), in_place(1))
        send(x_sems, 4 + q, chunk(sib.at[1], 2 + q), chunk(x_last.at[0], 2 + q), ahead)
        add(2, q, (), in_place(2))
        send(x_sems, 6 + q, chunk(sib.at[2], q), chunk(x_last.at[1], q), behind)
    partials(3)

    for way, dy, to in ((0, 1, right), (1, -1, left)):
        arrive(y_sems, way, y_first.at[way])
        for k in range(zh):
            own_part = term[way * zh + k, lax.rem(y + dy + NY, NY)].astype(f32)
            y_first[way, k] = (own_part + y_first[way, k].astype(f32)).astype(bf16)
        send(y_sems, 4 + way, y_first.at[way], y_half(y_last, way, way), to)
    for way in range(2):
        arrive(y_sems, 2 + way, y_half(y_last, way, 1 - way))
        arrive(y_sems, 4 + way, y_half(y_last, way, way))

    @pl.loop(0, nz)
    def _(i):
        at = lax.rem(z + i, nz)
        total = term[at, y].astype(f32) + y_last[0, at].astype(f32)
        y_sum[i] = (total + y_last[1, at].astype(f32)).astype(bf16)

    wide_row = y_sum.shape[2]
    cut = wide_row // (2 * LANES) * LANES
    halves = (pl.ds(0, cut), pl.ds(cut, wide_row - cut))
    send(z_sems, 0, y_sum.at[4, :, halves[0]], z_in.at[0, 0, :, halves[0]], up)
    send(z_sems, 1, y_sum.at[4, :, halves[1]], z_in.at[1, 0, :, halves[1]], down)

    for q in range(2):
        arrive(x_sems, q, x_first.at[0, pl.ds(q * quarter, quarter)])
        add(1, q, ((x_first.at[0], q * quarter),), in_place(1))
        send(x_sems, 8 + q, chunk(sib.at[1], q), chunk(x_last.at[0], q), ahead)
        arrive(x_sems, 2 + q, x_first.at[1, pl.ds(q * quarter, quarter)])
        add(2, 2 + q, ((x_first.at[1], q * quarter),), in_place(2))
        send(x_sems, 10 + q, chunk(sib.at[2], 2 + q), chunk(x_last.at[1], 2 + q), behind)

    for s in range(1, 4):
        for way, to in ((0, up), (1, down)):
            mine = 4 - s if way == 0 else 4 + s
            if s == 1:
                arrive(z_sems, way, z_in.at[way, 0, :, halves[way]])
                z_out[way, s] = y_sum[mine]
                both = y_sum[mine, :, halves[way]].astype(f32) + z_in[way, 0, :, halves[way]].astype(f32)
                z_out[way, s, :, halves[way]] = both.astype(bf16)
            else:
                arrive(z_sems, 2 * (s - 1) + way, z_in.at[way, s - 1])
                z_out[way, s] = (y_sum[mine].astype(f32) + z_in[way, s - 1].astype(f32)).astype(bf16)
            send(z_sems, 2 * s + way, z_out.at[way, s], z_in.at[way, s], to)
    for way in range(2):
        arrive(z_sems, 6 + way, z_in.at[way, 3])

    spread[...] = jnp.zeros_like(spread)
    for t in range(wide_row // LANES):
        at = pl.ds(t * LANES, LANES)
        total = y_sum[0, :, at].astype(f32) + z_in[0, 3, :, at].astype(f32)
        spread[:, t, :] = total + z_in[1, 3, :, at].astype(f32)
    for k in range(piece_rows):
        rows_out[k] = spread[k].astype(bf16)

    @pl.loop(0, n_ts)
    def _(h):
        pick = 0
        for k in range(1, piece_rows):
            pick = jnp.where(kept_ref[0, n_ts * k + me] // block == h, k, pick)
        slots_out[h] = rows_out[pick]

    def back_copy(step):
        to = lax.rem(me + step, n_ts)
        return pltpu.make_async_remote_copy(
            slots_out.at[to], back.at[me], b_send.at[step], b_recv.at[step],
            device_id={"ts": to}, device_id_type=MESH)

    @pl.loop(1, n_ts)
    def _(step):
        back_copy(step).start()

    back[me] = slots_out[me]

    def store_out(here, value):
        gate_ref[here, :] = value[:, :hid]
        up_ref[here, :] = value[:, hid : 2 * hid]
        down_ref[here, :] = value[:, 2 * hid :]

    def finish(q):
        for way in range(2):
            index = (8 + q, 6 + q)[way] if q < 2 else (2 + q, 8 + q)[way]
            arrive(x_sems, index, chunk(x_last.at[way], q))
        add(3, q, ((x_last.at[0], q * quarter), (x_last.at[1], q * quarter)), store_out)

    @pl.loop(1, n_ts)
    def _(step):
        source = lax.rem(me - step + n_ts, n_ts)
        pltpu.make_async_remote_copy(
            slots_out.at[source], back.at[source], b_send.at[step], b_recv.at[step],
            device_id={"ts": source}, device_id_type=MESH).wait_recv()

    @pl.loop(0, n_ts)
    def _(c):
        back_f[c] = back[c].astype(f32)

    for t in range(tiles):
        term_f[:, t * LANES:(t + 1) * LANES] = back_f[:, t, :]
    summed_dot = back_f[:, tiles, :][:, :1]
    own_f = own[...]
    own_inv = lax.rsqrt(jnp.sum(own_f * own_f, axis=1, keepdims=True) * (1.0 / width) + epsilon)
    own_weight = jax.nn.sigmoid(jnp.sum(own_f * scorer, axis=1, keepdims=True))
    unit = own_f * own_inv
    gained = term_f[...] * gain
    mean = jnp.sum(gained * unit, axis=1, keepdims=True) * (1.0 / width)
    row_grad = own_inv * (gained - unit * mean) + ((1.0 - own_weight) * summed_dot) * scorer
    token_ref[...] = dot(chosen, row_grad.astype(bf16)).astype(bf16)

    for q in range(4):
        finish(q)

    @pl.loop(1, n_ts)
    def _(step):
        p1_copy(step).wait_send()
        back_copy(step).wait_send()

    for copy in pending:
        copy.wait_send()


def local(
    block_activity, result_cotangent, kept_locations, prenormal_scaling, scorer_matrix,
    switch_matrix, expand_matrix, contract_matrix,
):
    n_ts, n_dp = lax.axis_size("ts"), lax.axis_size("dp")
    nz = n_ts // NY
    block, width = block_activity.shape[1:]
    cap = kept_locations.shape[1]
    hid = switch_matrix.shape[1]
    rows = width // n_dp
    piece = cap // n_ts
    tiles = width // LANES
    pad = -(-(tiles + 1) // 16) * 16
    bf16, f32, dma = jnp.bfloat16, jnp.float32, pltpu.SemaphoreType.DMA
    vmem = pl.BlockSpec(memory_space=pltpu.VMEM)
    hbm = pl.BlockSpec(memory_space=pl.ANY)
    token, gate, up, down = pl.pallas_call(
        functools.partial(block_kernel, n_ts, n_dp, (n_dp * cap) ** (-0.5)),
        out_shape=(
            jax.ShapeDtypeStruct((block, width), bf16),
            jax.ShapeDtypeStruct((rows, hid), bf16),
            jax.ShapeDtypeStruct((rows, hid), bf16),
            jax.ShapeDtypeStruct((hid, rows), bf16),
        ),
        in_specs=[pl.BlockSpec(memory_space=pltpu.SMEM)] + [vmem] * 5 + [hbm] * 3,
        out_specs=(vmem,) * 4,
        scratch_shapes=[
            pltpu.VMEM((width, hid), bf16), pltpu.VMEM((width, hid), bf16), pltpu.VMEM((hid, width), bf16), dma((3,)),
            pltpu.VMEM((n_ts, width), f32),
            pltpu.VMEM((n_ts, 2 * tiles, LANES), f32),
            pltpu.VMEM((n_ts, 2 * tiles, LANES), bf16),
            pltpu.VMEM((n_ts, 2 * tiles, LANES), bf16),
            pltpu.VMEM((piece, 2 * tiles, LANES), f32),
            pltpu.VMEM((piece, 2 * width), f32),
            pltpu.VMEM((2, n_ts, piece, width), bf16),
            dma((n_ts,)), dma((n_ts,)), dma((52,)), dma((52,)),
            pltpu.VMEM((cap, hid), f32), pltpu.VMEM((cap, hid), f32), pltpu.VMEM((cap, hid), f32),
            pltpu.VMEM((cap, hid), bf16), pltpu.VMEM((cap, hid), bf16), pltpu.VMEM((cap, 2 * hid), bf16),
            pltpu.VMEM((cap, hid), bf16),
            pltpu.VMEM((nz, NY, piece, width + LANES), bf16),
            pltpu.VMEM((4, 2 * rows, 3 * hid), bf16),
            pltpu.VMEM((4, rows, 3 * hid), bf16),
            pltpu.VMEM((2, rows // 2, 3 * hid), bf16),
            pltpu.VMEM((2, rows, 3 * hid), bf16),
            pltpu.VMEM((2, nz // 2, piece, width + LANES), bf16),
            pltpu.VMEM((2, nz, piece, width + LANES), bf16),
            pltpu.VMEM((nz, piece, width + LANES), bf16),
            pltpu.VMEM((2, 4, piece, width + LANES), bf16),
            pltpu.VMEM((2, 4, piece, width + LANES), bf16),
            pltpu.VMEM((piece, pad, LANES), f32),
            pltpu.VMEM((piece, pad, LANES), bf16),
            pltpu.VMEM((n_ts, pad, LANES), bf16),
            pltpu.VMEM((n_ts, pad, LANES), bf16),
            pltpu.VMEM((n_ts, pad, LANES), f32),
            pltpu.VMEM((n_ts, width), f32),
            dma((16,)), dma((16,)), dma((12,)), dma((12,)), dma((6,)), dma((6,)),
            dma((8,)), dma((8,)), dma((n_ts,)), dma((n_ts,)),
        ],
        compiler_params=pltpu.CompilerParams(
            collective_id=0, has_side_effects=True, vmem_limit_bytes=56 * 1024 * 1024),
        name="block_backward",
    )(
        kept_locations, kept_locations, block_activity[0], result_cotangent[0],
        prenormal_scaling[None], scorer_matrix[None], switch_matrix, expand_matrix, contract_matrix,
    )
    return (token[None], gate, up, down)


def solution(mesh):
    in_specs = (
        P("dp", "ts", None), P("dp", "ts", None), P("dp", None), P(), P(),
        P(None, "ts"), P(None, "ts"), P("ts", None),
    )
    out_specs = (P("dp", "ts", None), P("dp", "ts"), P("dp", "ts"), P("ts", "dp"))
    return jax.shard_map(local, mesh=mesh, in_specs=in_specs, out_specs=out_specs, check_vma=False)
```

time: 542 us -> 144 us (0.27)
  waiting for transfers between devices: 345 us -> 0 us
  Pallas kernels: 0 us -> 123 us
  blocking collectives: 71.9 us -> 0 us
  local copies, waits for them, and re-layouts: 54 us -> 19.4 us
  other arithmetic: 28.3 us -> 0 us
  matrix products: 22.3 us -> 0 us
  between operations: 16.6 us -> 0.64 us
    all_gather x2 -> x0, waiting for transfers between devices: 168 us -> none  [the longest x1 93.2 us: local(): lax.all_gather(own_rows, 'ts', axis=0, tiled=True)]
    pallas_call x0 -> x1, Pallas kernels: none -> 123 us  [local(): pl.pallas_call(functools.partial(block_kernel, n_ts, n_dp, (n_dp * cap) *...]
    reduce_scatter x1 -> x0, waiting for transfers between devices: 122 us -> none  [local(): lax.psum_scatter(term_pad.astype(jnp.bfloat16), 'ts', scatter_dimension=0...]
    unnamed x1 -> x0, blocking collectives: 71.9 us -> none
    unnamed x5 -> x0, waiting for transfers between devices: 55.5 us -> none
    dot_general x10 -> x0, matrix products: 22.3 us -> none  [the longest x1 4.91 us: local(): jnp.einsum('cd,fd->cf', scaled, contract_matrix, preferred_element_type=j...]
    gather x4 -> x0, local copies, waits for them, and re-layouts: 21.6 us -> none  [the longest x1 8.81 us: local(): row_data = jnp.take(all_rows, padded_pos, axis=0)]
    convert_element_type x5 -> x0, other arithmetic: 15.7 us -> none  [the longest x1 9.01 us: local(): term_pad.astype(jnp.bfloat16)]
  transfers between devices with their start and end apart: 4 -> 0, of which waited for: 4 -> 0; matrix products, arithmetic and copies ran while one was open for 10% -> 0% of each run, Pallas kernels for 0% -> 0%
where the time goes in v3:
time: 144 us; the launch traced here: 143 us
  Pallas kernels  123 us (85%)
  local copies, waits for them, and re-layouts  19.4 us (13%)
    pallas_call x1, Pallas kernels, local(): pl.pallas_call(functools.partial(block_kernel, n_ts, n_dp, (n_dp * cap) *...  123 us
    unnamed x8, local copies, waits for them, and re-layouts  16.8 us

profile of v3, /device:TPU:2, one launch (start us, length us, event | category | flops | bytes accessed | tf_op | source)
XLA Modules:
  0.0 143.3 jit_solution(15824871660688873774)
XLA Ops:
  0.6 1.3 broadcast_in_dim.9.gain_ref
  1.9 1.3 broadcast_in_dim.10.scorer_ref
  3.2 0.0 copy-start
  3.2 5.9 %copy.12.switch_hbm = bf16[3584,448]{1,0:T(8,128)(2,1)} copy(bf16[3584,448]{0,1:T(8,128)(2,1)} %param.13) | data formatting | bytes 6422528 | tf_op args[5]
  9.1 0.0 copy-done
  9.1 3.6 %copy.13.expand_hbm = bf16[3584,448]{1,0:T(8,128)(2,1)} copy(bf16[3584,448]{0,1:T(8,128)(2,1)S(1)} %copy-done) | data formatting | bytes 6422528 | tf_op args[6]
  12.8 123.2 %block_backward.1 = (bf16[64,3584]{1,0:T(8,128)(2,1)}, bf16[448,448]{1,0:T(8,128)(2,1)}, bf16[448,448]{1,0:T(8,128)(2,1)}, bf16[448,448]{1,0:T(8,128)(2,1)}) custom-call(s32[1,256]{1,0:T(1,128)} %kept_row.1, s32[1,256]{1,0:T(1,128)} %kept_row.1, bf16[64,3584]{1,0:T(8,128)(2,1)} %bitcast.4, bf16[64,3584]{1,0:T(8,128)(2,1)} %bitcast.5, ...), custom_call_target="tpu_custom_call" | custom-call | tf_op jit(solution)/shard_map/block_backward/pallas_call | solution.py:499
  136.0 1.8 %copy.18 = bf16[1,64,3584]{2,1,0:T(8,128)(2,1)} copy(bf16[1,64,3584]{2,1,0:T(8,128)(2,1)} %bitcast.3) | data formatting | bytes 917504
  137.8 1.8 %copy.19 = bf16[448,448]{1,0:T(8,128)(2,1)} copy(bf16[448,448]{1,0:T(8,128)(2,1)} %get-tuple-element.17) | data formatting | bytes 802816
  139.7 1.8 %copy.20 = bf16[448,448]{1,0:T(8,128)(2,1)} copy(bf16[448,448]{1,0:T(8,128)(2,1)} %get-tuple-element.18) | data formatting | bytes 802816
  141.5 1.8 %copy.21 = bf16[448,448]{1,0:T(8,128)(2,1)} copy(bf16[448,448]{1,0:T(8,128)(2,1)} %get-tuple-element.19) | data formatting | bytes 802816
Async XLA Ops:
  3.2 5.9 %copy-start = (bf16[3584,448]{0,1:T(8,128)(2,1)S(1)}, bf16[3584,448]{0,1:T(8,128)(2,1)}, u32[]{:S(2)}) copy-start(bf16[3584,448]{0,1:T(8,128)(2,1)} %param.14) | copy-start | bytes 9633796

commit v4 on v3

v4 whole, which is shorter than its diff:
```python
import functools
import math

import jax
import jax.numpy as jnp
from jax import lax
from jax.experimental import pallas as pl
from jax.experimental.pallas import tpu as pltpu
from jax.sharding import PartitionSpec as P

MESH = pl.DeviceIdType.MESH
NY = 4
RS_ORDER = (
    "acts_start", "terms", ("y", 4), ("y", 3), ("y", 5), ("p", 0), ("p", 1), ("p", 2), ("p", 3), ("s", 4), "acts_relay",
    ("y", 2), ("y", 6), "x_start", ("s", 3), ("s", 5), ("e", 4), ("z", 0), ("y", 1), ("y", 7), "seen_end", "grow_own",
    ("s", 2), ("s", 6), ("e", 3), ("e", 5), ("z", 1), ("y", 0), "acts_near", ("s", 1), ("s", 7), ("e", 2), ("e", 6),
    ("z", 2), ("s", 0), "grow_near", ("e", 1), ("e", 7), ("z", 3), "acts_far", ("e", 0), "x_second", "back_start",
    "grow_far", "back_end", "x_end",
)
AG_ORDER = (
    "b1_start", "a1_start", ("f", 0), "b1_relay", ("a", 1), "b1_end", "b2_start", ("a", 2), ("r", 0), ("a", 3),
    ("r", 1), ("l", 0), ("n", 0), ("r", 2), ("g", 1), ("l", 1), ("n", 1), ("a", 4), ("r", 3), ("l", 2), ("n", 2),
    ("r", 4), ("g", 2), ("l", 3), ("n", 3), ("r", 5), ("l", 4), ("n", 4), ("r", 6), ("l", 5), ("n", 5),
    ("r", 7), ("l", 6), ("n", 6), ("g", 3), ("l", 7), ("n", 7), ("g", 4),
)
Z_STEPS = (0, -1, 1, -2, 2, -3, 3, 4)
LANES = 128
K_TILE = 512
epsilon = 1e-06
gelu_scale = math.sqrt(2.0 / math.pi)
ROWS_BY_ROWS = (((0,), (0,)), ((), ()))
COLS_BY_COLS = (((1,), (1,)), ((), ()))


def gelu_pair(pre_act):
    cubic = pre_act + 0.044715 * pre_act * pre_act * pre_act
    tanh_part = jnp.tanh(gelu_scale * cubic)
    gelu_out = 0.5 * pre_act * (1.0 + tanh_part)
    slope_out = 0.5 * (1.0 + tanh_part) + 0.5 * pre_act * (
        1.0 - tanh_part * tanh_part
    ) * gelu_scale * (1.0 + 3.0 * 0.044715 * pre_act * pre_act)
    return (gelu_out, slope_out)


def dot(a, b, dims=(((1,), (0,)), ((), ()))):
    return lax.dot_general(a, b, dims, preferred_element_type=jnp.float32)


def block_kernel(
    n_ts, n_dp, factor,
    kept_ref, kept_row, act_ref, cot_ref, vectors_ref, switch_hbm, expand_hbm, contract_hbm,
    token_ref, gate_ref, up_ref, down_ref,
    switch, expand, contract, w_sem,
    own, slots_f, slots, landed, wide, piece_f, zy, yz, scaled, p1_send, p1_recv, g_send, g_recv,
    pre_gate, pre_up, hidden_grad, gate_in, up_in, acts, hidden, term,
    pair, sib, x_first, x_last, y_first, y_last, y_sum, z_in, z_out, spread, rows_out, slots_out, back, back_f, term_f,
    sib_send, sib_recv, seen, total, n_send, n_recv, a_send, a_recv, x_send, x_recv, y_send, y_recv, z_send, z_recv, b_send, b_recv,
):
    bf16, f32 = jnp.bfloat16, jnp.float32
    nz = n_ts // NY
    nx = n_dp // 2
    me = lax.axis_index("ts")
    z, y = me // NY, lax.rem(me, NY)
    dp = lax.axis_index("dp")
    x, core = dp // 2, lax.rem(dp, 2)
    block, width = act_ref.shape
    tiles = width // LANES
    piece_rows = zy.shape[1]
    cap = n_ts * piece_rows
    hid = hidden.shape[1]
    pending = []

    def node(dz, dy):
        return lax.rem(z + dz + nz, nz) * NY + lax.rem(y + dy + NY, NY)

    def chip(dx):
        return lax.rem(x + dx + nx, nx) * 2 + core

    def copy_to(sems, index, src, dst, where):
        return pltpu.make_async_remote_copy(
            src, dst, sems[0].at[index], sems[1].at[index], device_id=where, device_id_type=MESH)

    def send(sems, index, src, dst, where):
        copy = copy_to(sems, index, src, dst, where)
        copy.start()
        pending.append(copy)

    def arrive(sems, index, dst):
        copy_to(sems, index, dst, dst, {"ts": me}).wait_recv()

    right, left = {"ts": node(0, 1)}, {"ts": node(0, -1)}
    up, down = {"ts": node(1, 0)}, {"ts": node(-1, 0)}
    ahead, behind = {"dp": chip(1)}, {"dp": chip(-1)}
    sibling = {"dp": x * 2 + 1 - core}

    barrier = pltpu.get_barrier_semaphore()

    @pl.loop(1, n_ts)
    def _(step):
        pl.semaphore_signal(barrier, inc=1, device_id={"ts": lax.rem(me + step, n_ts)}, device_id_type=MESH)

    @pl.loop(1, n_dp)
    def _(step):
        pl.semaphore_signal(barrier, inc=1, device_id={"dp": lax.rem(dp + step, n_dp)}, device_id_type=MESH)

    weight_copies = [
        pltpu.make_async_copy(src, dst, w_sem.at[i])
        for i, (src, dst) in enumerate(((switch_hbm, switch), (expand_hbm, expand), (contract_hbm, contract)))
    ]
    for copy in weight_copies:
        copy.start()

    kept = jnp.broadcast_to(kept_row[...], (block, cap))
    position = lax.broadcasted_iota(jnp.int32, (block, cap), 0) + block * me
    rank = jnp.sum((kept < position).astype(f32), axis=1, keepdims=True)
    routed = jnp.sum((kept == position).astype(f32), axis=1, keepdims=True)
    row_class = rank - n_ts * jnp.floor(rank * (1.0 / n_ts))
    classes = lax.broadcasted_iota(jnp.int32, (block, n_ts), 1).astype(f32)
    chosen = jnp.where(classes == row_class, routed, 0.0).astype(bf16)
    own[...] = dot(chosen, act_ref[...], ROWS_BY_ROWS)
    own_cot = dot(chosen, cot_ref[...], ROWS_BY_ROWS)
    for t in range(tiles):
        slots_f[:, t, :] = own[:, t * LANES:(t + 1) * LANES]
        slots_f[:, tiles + t, :] = own_cot[:, t * LANES:(t + 1) * LANES]

    @pl.loop(0, n_ts)
    def _(c):
        slots[c] = slots_f[c].astype(bf16)

    pl.semaphore_wait(barrier, n_ts - 1 + n_dp - 1)


    def p1_copy(step):
        to = lax.rem(me + step, n_ts)
        return pltpu.make_async_remote_copy(
            slots.at[to], landed.at[me], p1_send.at[step], p1_recv.at[step],
            device_id={"ts": to}, device_id_type=MESH)

    @pl.loop(1, n_ts)
    def _(step):
        p1_copy(step).start()

    landed[me] = slots[me]

    @pl.loop(1, n_ts)
    def _(step):
        source = lax.rem(me - step + n_ts, n_ts)
        pltpu.make_async_remote_copy(
            slots.at[source], landed.at[source], p1_send.at[step], p1_recv.at[step],
            device_id={"ts": source}, device_id_type=MESH).wait_recv()


    for k in range(piece_rows):
        wide[k] = landed[kept_ref[0, n_ts * k + me] // block].astype(f32)
    for t in range(2 * tiles):
        piece_f[:, t * LANES:(t + 1) * LANES] = wide[:, t, :]

    gain = vectors_ref[0:1, :].astype(f32)
    scorer = vectors_ref[1:2, :].astype(f32)
    row_f = piece_f[:, :width]
    inv_rms = lax.rsqrt(jnp.sum(row_f * row_f, axis=1, keepdims=True) * (1.0 / width) + epsilon)
    weight = jax.nn.sigmoid(jnp.sum(row_f * scorer, axis=1, keepdims=True))
    zy[me, :, :width] = (row_f * inv_rms * gain).astype(bf16)
    scaled_rows = (weight * piece_f[:, width:]).astype(bf16)
    yz[me] = scaled_rows[:, : yz.shape[2]]
    zy[me, :, width:] = scaled_rows[:, yz.shape[2] :]


    g_sems = (g_send, g_recv)

    def cut(buffer, which):
        first = -(-buffer.shape[2] // (2 * LANES)) * LANES
        return pl.ds(0, first) if which == 0 else pl.ds(first, buffer.shape[2] - first)

    def piece(buffer, n, which=None):
        return buffer.at[n] if which is None else buffer.at[n, :, cut(buffer, which)]

    def group(dz, which):
        return yz.at[pl.ds(lax.rem(z + dz + nz, nz) * NY + which * (NY // 2), NY // 2)]

    def share(index, ref, where):
        send(g_sems, index, ref, ref, where)

    B1, A1, B2, A2, A3 = 0, 4, 12, 26, 42

    def b1_start():
        share(B1 + 0, piece(yz, me), right)
        share(B1 + 1, piece(yz, me), left)

    def b1_relay():
        arrive(g_sems, B1 + 0, piece(yz, node(0, -1)))
        share(B1 + 2, piece(yz, node(0, -1), 0), right)
        arrive(g_sems, B1 + 1, piece(yz, node(0, 1)))
        share(B1 + 3, piece(yz, node(0, 1), 1), left)

    def b1_end():
        arrive(g_sems, B1 + 2, piece(yz, node(0, -2), 0))
        arrive(g_sems, B1 + 3, piece(yz, node(0, 2), 1))

    def a1_start():
        share(A1 + 0, piece(zy, me), up)
        share(A1 + 1, piece(zy, me), down)

    def fan_out(j):
        dz = Z_STEPS[j]
        share(A2 + 2 * j, piece(zy, node(dz, 0)), right)
        share(A2 + 2 * j + 1, piece(zy, node(dz, 0)), left)

    def relay(j):
        dz = Z_STEPS[j]
        arrive(g_sems, A2 + 2 * j, piece(zy, node(dz, -1)))
        share(A3 + 2 * j, piece(zy, node(dz, -1), 0), right)
        arrive(g_sems, A2 + 2 * j + 1, piece(zy, node(dz, 1)))
        share(A3 + 2 * j + 1, piece(zy, node(dz, 1), 1), left)

    def last(j):
        arrive(g_sems, A3 + 2 * j, piece(zy, node(Z_STEPS[j], -2), 0))
        arrive(g_sems, A3 + 2 * j + 1, piece(zy, node(Z_STEPS[j], 2), 1))

    def along(s):
        which = (0, 1) if s == 4 else (None, None)
        further = (0, 1) if s == 3 else (None, None)
        for way, to, sign in ((0, up, -1), (1, down, 1)):
            arrive(g_sems, A1 + 2 * (s - 1) + way, piece(zy, node(sign * s, 0), which[way]))
            if s < 4:
                share(A1 + 2 * s + way, piece(zy, node(sign * s, 0), further[way]), to)
        if s < 4:
            fan_out(2 * s - 1)
            fan_out(2 * s)
        else:
            fan_out(7)

    def b2_start():
        for which in range(2):
            share(B2 + 2 * which, group(0, which), up)
            share(B2 + 2 * which + 1, group(0, which), down)

    def groups(s):
        for which in range(2):
            for way, to, sign in ((0, up, -1), (1, down, 1)):
                if s == 4 and way != which:
                    continue
                index = B2 + 12 + way if s == 4 else B2 + 4 * (s - 1) + 2 * which + way
                arrive(g_sems, index, group(sign * s, which))
                if s < 3:
                    share(B2 + 4 * s + 2 * which + way, group(sign * s, which), to)
                elif s == 3 and way == which:
                    share(B2 + 12 + way, group(sign * s, which), to)

    window = seen.shape[3]
    pair_width = 2 * width // n_dp

    def window_at(to):
        return pl.multiple_of(to // 2 * pair_width + lax.rem(to, 2) * (pair_width - window), LANES)

    def seen_copy(j, step):
        n = pl.ds(lax.rem(z + Z_STEPS[j] + nz, nz) * NY, NY)
        to = lax.rem(dp + step, n_dp)
        index = (step - 1) * nz + j
        return pltpu.make_async_remote_copy(
            zy.at[n, :, pl.ds(window_at(to), window)], seen.at[dp, n], n_send.at[index], n_recv.at[index],
            device_id={"dp": to}, device_id_type=MESH)

    def show(j):
        @pl.loop(1, n_dp)
        def _(step):
            seen_copy(j, step).start()

    def seen_wait(j):
        n = pl.ds(lax.rem(z + Z_STEPS[j] + nz, nz) * NY, NY)

        @pl.loop(1, n_dp)
        def _(step):
            index = (step - 1) * nz + j
            source = lax.rem(dp - step + n_dp, n_dp)
            arrive((n_send, n_recv), index, seen.at[source, n])
            seen_copy(j, step).wait_send()

    steps = dict(
        b1_start=b1_start, b1_relay=b1_relay, b1_end=b1_end, a1_start=a1_start, b2_start=b2_start)
    for step in AG_ORDER:
        if isinstance(step, str):
            steps[step]()
        else:
            (fan_out, relay, last, along, groups, show)["frlagn".index(step[0])](step[1])

    def columns(buffer, start, size):
        return buffer[:, :, pl.ds(start, size)].reshape(cap, size)


    for copy in weight_copies:
        copy.wait()
    pre_gate[...] = jnp.zeros_like(pre_gate)
    pre_up[...] = jnp.zeros_like(pre_up)
    hidden_grad[...] = jnp.zeros_like(hidden_grad)

    @pl.loop(0, width // K_TILE)
    def _(k):
        at = pl.ds(pl.multiple_of(k * K_TILE, K_TILE), K_TILE)
        normed = columns(zy, pl.multiple_of(k * K_TILE, K_TILE), K_TILE)
        pre_gate[...] += dot(normed, switch[:, at], COLS_BY_COLS)
        pre_up[...] += dot(normed, expand[:, at], COLS_BY_COLS)

    for p in range(n_dp // 2):
        at = pl.ds(p * pair_width, pair_width)
        if p < n_dp // 2 - 1:
            scaled[:, at] = columns(yz, p * pair_width, pair_width)
        else:
            scaled[:, at] = columns(zy, width, pair_width)
        hidden_grad[...] += dot(scaled[:, at], contract[:, at], COLS_BY_COLS)

    @pl.loop(0, nz)
    def _(i):
        n = cap // nz
        at = pl.ds(pl.multiple_of(i * n, n), n)
        gelu_out, slope_out = gelu_pair(pre_gate[at, :])
        up_value, grad = pre_up[at, :], hidden_grad[at, :]
        hidden_value = (gelu_out * up_value).astype(bf16)
        hidden[at, :] = hidden_value
        gate_value = (grad * up_value * slope_out).astype(bf16)
        up_back = (grad * gelu_out).astype(bf16)
        gate_in[at, :] = gate_value
        up_in[at, :] = up_back
        acts[dp, at, :hid] = gate_value
        acts[dp, at, hid:] = up_back
        router = jnp.sum(hidden_value.astype(f32) * grad, axis=1, keepdims=True)
        term[i, :, :, width:] = jnp.broadcast_to(router, (n, LANES)).astype(bf16).reshape(NY, piece_rows, LANES)


    a_sems = (a_send, a_recv)
    halves = (pl.ds(0, cap // 2), pl.ds(cap // 2, cap // 2))

    def other(dx):
        return lax.rem(x + dx + nx, nx) * 2 + 1 - core

    def part(q, which):
        return acts.at[q, halves[which]]

    def pass_on(index, ref, where):
        send(a_sems, index, ref, ref, where)

    def acts_start():
        pass_on(0, part(dp, 0), ahead)
        pass_on(2, part(dp, 1), behind)
        pass_on(1, part(dp, 1), ahead)
        pass_on(3, part(dp, 0), behind)
        pass_on(6, acts.at[dp], sibling)

    def acts_relay():
        arrive(a_sems, 0, part(chip(-1), 0))
        pass_on(4, part(chip(-1), 0), ahead)
        pass_on(7, part(chip(-1), 0), sibling)
        arrive(a_sems, 2, part(chip(1), 1))
        pass_on(5, part(chip(1), 1), behind)
        pass_on(10, part(chip(1), 1), sibling)

    def acts_near():
        arrive(a_sems, 1, part(chip(-1), 1))
        pass_on(8, part(chip(-1), 1), sibling)
        arrive(a_sems, 3, part(chip(1), 0))
        pass_on(9, part(chip(1), 0), sibling)

    def acts_far():
        arrive(a_sems, 4, part(chip(2), 0))
        pass_on(11, part(chip(2), 0), sibling)
        arrive(a_sems, 5, part(chip(2), 1))
        pass_on(12, part(chip(2), 1), sibling)

    def grow(q):
        total[...] += dot(seen[q].reshape(cap, window), acts[q], ROWS_BY_ROWS)

    def grow_own():
        total[...] = dot(columns(zy, window_at(dp), window), acts[dp], ROWS_BY_ROWS)
        arrive(a_sems, 6, acts.at[other(0)])
        grow(other(0))

    def grow_near():
        for dx, index in ((-1, 7), (1, 9)):
            grow(chip(dx))
            arrive(a_sems, index, part(other(dx), 0))
            arrive(a_sems, index + 1, part(other(dx), 1))
            grow(other(dx))

    def grow_far():
        grow(chip(2))
        arrive(a_sems, 11, part(other(2), 0))
        arrive(a_sems, 12, part(other(2), 1))
        grow(other(2))
        here = pl.ds(pl.multiple_of(core * (window - rows), 8), rows)
        gate_ref[...] = (factor * total[here, :hid]).astype(bf16)
        up_ref[...] = (factor * total[here, hid:]).astype(bf16)

    sib_sems, x_sems, y_sems = (sib_send, sib_recv), (x_send, x_recv), (y_send, y_recv)
    z_sems = (z_send, z_recv)
    rows = width // n_dp
    quarter = hid // 4
    order = (2, 1, -1, 0)

    def partials(j):
        start = pl.multiple_of(lax.rem(x + order[j] + nx, nx) * pair_width, LANES)
        both = (factor * dot(hidden[...], scaled[:, pl.ds(start, pair_width)], ROWS_BY_ROWS)).astype(bf16)
        pair[j, 0] = both[:, :rows]
        pair[j, 1] = both[:, rows:]
        for q in range(4):
            at = pl.ds(q * quarter, quarter)
            send(sib_sems, 4 * j + q, pair.at[j, 1 - core, at], sib.at[j, at], sibling)

    def add(j, q, others, store):
        arrive(sib_sems, 4 * j + q, sib.at[j, pl.ds(q * quarter, quarter)])
        here = pl.ds(q * quarter, quarter)
        value = pair[j, core, here, :].astype(f32) + sib[j, here, :].astype(f32)
        for ref, start in others:
            value += ref[pl.ds(start, quarter), :].astype(f32)
        store(here, value.astype(bf16))

    def in_place(j):
        def store(here, value):
            sib[j, here, :] = value
        return store

    def chunk(ref, q):
        return ref.at[pl.ds(q * quarter, quarter)]

    def x_start():
        for q in (0, 2, 1, 3):
            add(0, q, (), in_place(0))
            way = q // 2
            send(x_sems, q, chunk(sib.at[0], q), x_first.at[way, pl.ds((q % 2) * quarter, quarter)],
                 (ahead, behind)[way])
        for q in range(2):
            add(1, 2 + q, (), in_place(1))
            send(x_sems, 4 + q, chunk(sib.at[1], 2 + q), chunk(x_last.at[0], 2 + q), ahead)
            add(2, q, (), in_place(2))
            send(x_sems, 6 + q, chunk(sib.at[2], q), chunk(x_last.at[1], q), behind)

    def x_second():
        for q in range(2):
            arrive(x_sems, q, x_first.at[0, pl.ds(q * quarter, quarter)])
            add(1, q, ((x_first.at[0], q * quarter),), in_place(1))
            send(x_sems, 8 + q, chunk(sib.at[1], q), chunk(x_last.at[0], q), ahead)
            arrive(x_sems, 2 + q, x_first.at[1, pl.ds(q * quarter, quarter)])
            add(2, 2 + q, ((x_first.at[1], q * quarter),), in_place(2))
            send(x_sems, 10 + q, chunk(sib.at[2], 2 + q), chunk(x_last.at[1], 2 + q), behind)

    def x_end():
        def store_out(here, value):
            down_ref[here, :] = value

        for q in (2, 3, 0, 1):
            for way in range(2):
                index = (8 + q, 6 + q)[way] if q < 2 else (2 + q, 8 + q)[way]
                arrive(x_sems, index, chunk(x_last.at[way], q))
            add(3, q, ((x_last.at[0], q * quarter), (x_last.at[1], q * quarter)), store_out)

    wide_row = y_sum.shape[2]
    middle = -(-wide_row // (2 * LANES)) * LANES
    cols = (pl.ds(0, middle), pl.ds(middle, wide_row - middle))

    def terms():
        @pl.loop(0, width // K_TILE)
        def _(k):
            at = pl.ds(pl.multiple_of(k * K_TILE, K_TILE), K_TILE)
            value = dot(gate_in[...], switch[:, at]) + dot(up_in[...], expand[:, at])
            term[:, :, :, at] = value.astype(bf16).reshape(nz, NY, piece_rows, K_TILE)

    def at_z(i):
        return lax.rem(z + i, nz)

    def at_y(dy):
        return lax.rem(y + dy + NY, NY)

    def y_start(i):
        opposite = term.at[at_z(i), at_y(2)]
        send(y_sems, 6 * i, opposite.at[:, cols[0]], y_first.at[i, :, cols[0]], right)
        send(y_sems, 6 * i + 1, opposite.at[:, cols[1]], y_first.at[i, :, cols[1]], left)
        send(y_sems, 6 * i + 2, term.at[at_z(i), at_y(1), :, cols[1]], y_last.at[0, i, :, cols[1]], right)
        send(y_sems, 6 * i + 3, term.at[at_z(i), at_y(-1), :, cols[0]], y_last.at[1, i, :, cols[0]], left)

    def y_second(i):
        for way, dy, to in ((0, 1, right), (1, -1, left)):
            arrive(y_sems, 6 * i + way, y_first.at[i, :, cols[way]])
            value = term[at_z(i), at_y(dy), :, cols[way]].astype(f32) + y_first[i, :, cols[way]].astype(f32)
            y_first[i, :, cols[way]] = value.astype(bf16)
            send(y_sems, 6 * i + 4 + way, y_first.at[i, :, cols[way]], y_last.at[way, i, :, cols[way]], to)

    def y_end(i):
        for way in range(2):
            arrive(y_sems, 6 * i + 2 + way, y_last.at[way, i, :, cols[1 - way]])
            arrive(y_sems, 6 * i + 4 + way, y_last.at[way, i, :, cols[way]])
        value = term[at_z(i), y].astype(f32) + y_last[0, i].astype(f32)
        y_sum[i] = (value + y_last[1, i].astype(f32)).astype(bf16)

    def z_step(s):
        for way, to in ((0, up), (1, down)):
            mine = 4 - s if way == 0 else 4 + s
            if s == 0:
                send(z_sems, way, y_sum.at[4, :, cols[way]], z_in.at[way, 0, :, cols[way]], to)
                continue
            if s == 1:
                arrive(z_sems, way, z_in.at[way, 0, :, cols[way]])
                z_out[way, s] = y_sum[mine]
                both = y_sum[mine, :, cols[way]].astype(f32) + z_in[way, 0, :, cols[way]].astype(f32)
                z_out[way, s, :, cols[way]] = both.astype(bf16)
            else:
                arrive(z_sems, 2 * (s - 1) + way, z_in.at[way, s - 1])
                z_out[way, s] = (y_sum[mine].astype(f32) + z_in[way, s - 1].astype(f32)).astype(bf16)
            send(z_sems, 2 * s + way, z_out.at[way, s], z_in.at[way, s], to)

    def back_copy(step):
        to = lax.rem(me + step, n_ts)
        return pltpu.make_async_remote_copy(
            slots_out.at[to], back.at[me], b_send.at[step], b_recv.at[step],
            device_id={"ts": to}, device_id_type=MESH)

    def back_start():
        for way in range(2):
            arrive(z_sems, 6 + way, z_in.at[way, 3])
        spread[...] = jnp.zeros_like(spread)
        for t in range(wide_row // LANES):
            at = pl.ds(t * LANES, LANES)
            value = y_sum[0, :, at].astype(f32) + z_in[0, 3, :, at].astype(f32)
            spread[:, t, :] = value + z_in[1, 3, :, at].astype(f32)
        for k in range(piece_rows):
            rows_out[k] = spread[k].astype(bf16)

        @pl.loop(0, n_ts)
        def _(h):
            pick = 0
            for k in range(1, piece_rows):
                pick = jnp.where(kept_ref[0, n_ts * k + me] // block == h, k, pick)
            slots_out[h] = rows_out[pick]

        @pl.loop(1, n_ts)
        def _(step):
            back_copy(step).start()

        back[me] = slots_out[me]

    def back_end():
        @pl.loop(1, n_ts)
        def _(step):
            source = lax.rem(me - step + n_ts, n_ts)
            pltpu.make_async_remote_copy(
                slots_out.at[source], back.at[source], b_send.at[step], b_recv.at[step],
                device_id={"ts": source}, device_id_type=MESH).wait_recv()

        @pl.loop(0, n_ts)
        def _(c):
            back_f[c] = back[c].astype(f32)

        for t in range(tiles):
            term_f[:, t * LANES:(t + 1) * LANES] = back_f[:, t, :]
        summed_dot = back_f[:, tiles, :][:, :1]
        own_f = own[...]
        own_inv = lax.rsqrt(jnp.sum(own_f * own_f, axis=1, keepdims=True) * (1.0 / width) + epsilon)
        own_weight = jax.nn.sigmoid(jnp.sum(own_f * scorer, axis=1, keepdims=True))
        unit = own_f * own_inv
        gained = term_f[...] * gain
        mean = jnp.sum(gained * unit, axis=1, keepdims=True) * (1.0 / width)
        row_grad = own_inv * (gained - unit * mean) + ((1.0 - own_weight) * summed_dot) * scorer
        token_ref[...] = dot(chosen, row_grad.astype(bf16)).astype(bf16)

    def seen_end():
        for j in range(nz):
            seen_wait(j)

    jobs = dict(
        acts_start=acts_start, acts_relay=acts_relay, acts_near=acts_near, acts_far=acts_far, grow_own=grow_own,
        grow_near=grow_near, grow_far=grow_far, x_start=x_start, x_second=x_second, x_end=x_end, terms=terms,
        back_start=back_start, back_end=back_end, seen_end=seen_end)
    for job in RS_ORDER:
        if isinstance(job, str):
            jobs[job]()
        else:
            (partials, y_start, y_second, y_end, z_step)["pysez".index(job[0])](job[1])

    @pl.loop(1, n_ts)
    def _(step):
        p1_copy(step).wait_send()
        back_copy(step).wait_send()

    for copy in pending:
        copy.wait_send()


def store_kernel(*refs):
    sems = refs[-1]
    count = (len(refs) - 1) // 2
    copies = [pltpu.make_async_copy(refs[i], refs[count + i], sems.at[i]) for i in range(count)]
    for copy in copies:
        copy.start()
    for copy in copies:
        copy.wait()


def store_results(*results):
    hbm = pl.BlockSpec(memory_space=pl.ANY)
    return pl.pallas_call(
        store_kernel,
        out_shape=tuple(jax.ShapeDtypeStruct(r.shape, r.dtype) for r in results),
        in_specs=[hbm] * len(results),
        out_specs=(hbm,) * len(results),
        scratch_shapes=[pltpu.SemaphoreType.DMA((len(results),))],
        name="store_results",
    )(*results)


def local(
    block_activity, result_cotangent, kept_locations, prenormal_scaling, scorer_matrix,
    switch_matrix, expand_matrix, contract_matrix,
):
    n_ts, n_dp = lax.axis_size("ts"), lax.axis_size("dp")
    nz = n_ts // NY
    block, width = block_activity.shape[1:]
    cap = kept_locations.shape[1]
    hid = switch_matrix.shape[1]
    rows = width // n_dp
    piece = cap // n_ts
    tiles = width // LANES
    window = -(-rows // LANES) * LANES
    pad = -(-(tiles + 1) // 16) * 16
    bf16, f32, dma = jnp.bfloat16, jnp.float32, pltpu.SemaphoreType.DMA
    vmem = pl.BlockSpec(memory_space=pltpu.VMEM)
    hbm = pl.BlockSpec(memory_space=pl.ANY)
    token, gate, up, down = pl.pallas_call(
        functools.partial(block_kernel, n_ts, n_dp, (n_dp * cap) ** (-0.5)),
        out_shape=(
            jax.ShapeDtypeStruct((block, width), bf16),
            jax.ShapeDtypeStruct((rows, hid), bf16),
            jax.ShapeDtypeStruct((rows, hid), bf16),
            jax.ShapeDtypeStruct((hid, rows), bf16),
        ),
        in_specs=[pl.BlockSpec(memory_space=pltpu.SMEM)] + [vmem] * 4 + [hbm] * 3,
        out_specs=(vmem,) * 4,
        scratch_shapes=[
            pltpu.VMEM((hid, width), bf16), pltpu.VMEM((hid, width), bf16), pltpu.VMEM((hid, width), bf16), dma((3,)),
            pltpu.VMEM((n_ts, width), f32),
            pltpu.VMEM((n_ts, 2 * tiles, LANES), f32),
            pltpu.VMEM((n_ts, 2 * tiles, LANES), bf16),
            pltpu.VMEM((n_ts, 2 * tiles, LANES), bf16),
            pltpu.VMEM((piece, 2 * tiles, LANES), f32),
            pltpu.VMEM((piece, 2 * width), f32),
            pltpu.VMEM((n_ts, piece, width + 2 * rows), bf16),
            pltpu.VMEM((n_ts, piece, width - 2 * rows), bf16),
            pltpu.VMEM((cap, width), bf16),
            dma((n_ts,)), dma((n_ts,)), dma((58,)), dma((58,)),
            pltpu.VMEM((cap, hid), f32), pltpu.VMEM((cap, hid), f32), pltpu.VMEM((cap, hid), f32),
            pltpu.VMEM((cap, hid), bf16), pltpu.VMEM((cap, hid), bf16), pltpu.VMEM((n_dp, cap, 2 * hid), bf16),
            pltpu.VMEM((cap, hid), bf16),
            pltpu.VMEM((nz, NY, piece, width + LANES), bf16),
            pltpu.VMEM((4, 2, hid, rows), bf16),
            pltpu.VMEM((4, hid, rows), bf16),
            pltpu.VMEM((2, hid // 2, rows), bf16),
            pltpu.VMEM((2, hid, rows), bf16),
            pltpu.VMEM((nz, piece, width + LANES), bf16),
            pltpu.VMEM((2, nz, piece, width + LANES), bf16),
            pltpu.VMEM((nz, piece, width + LANES), bf16),
            pltpu.VMEM((2, 4, piece, width + LANES), bf16),
            pltpu.VMEM((2, 4, piece, width + LANES), bf16),
            pltpu.VMEM((piece, pad, LANES), f32),
            pltpu.VMEM((piece, pad, LANES), bf16),
            pltpu.VMEM((n_ts, pad, LANES), bf16),
            pltpu.VMEM((n_ts, pad, LANES), bf16),
            pltpu.VMEM((n_ts, pad, LANES), f32),
            pltpu.VMEM((n_ts, width), f32),
            dma((16,)), dma((16,)),
            pltpu.VMEM((n_dp, n_ts, piece, window), bf16),
            pltpu.VMEM((window, 2 * hid), f32),
            dma((n_dp * nz,)), dma((n_dp * nz,)), dma((13,)), dma((13,)),
            dma((12,)), dma((12,)), dma((6 * nz,)), dma((6 * nz,)),
            dma((8,)), dma((8,)), dma((n_ts,)), dma((n_ts,)),
        ],
        compiler_params=pltpu.CompilerParams(
            collective_id=0, has_side_effects=True, vmem_limit_bytes=56 * 1024 * 1024),
        name="block_backward",
    )(
        kept_locations, kept_locations, block_activity[0], result_cotangent[0],
        jnp.stack([prenormal_scaling, scorer_matrix]), switch_matrix.T, expand_matrix.T, contract_matrix,
    )
    return store_results(token[None], gate, up, down)


def solution(mesh):
    in_specs = (
        P("dp", "ts", None), P("dp", "ts", None), P("dp", None), P(), P(),
        P(None, "ts"), P(None, "ts"), P("ts", None),
    )
    out_specs = (P("dp", "ts", None), P("dp", "ts"), P("dp", "ts"), P("ts", "dp"))
    return jax.shard_map(local, mesh=mesh, in_specs=in_specs, out_specs=out_specs, check_vma=False)
```

time: 144 us -> 167 us (1.16)
  Pallas kernels: 123 us -> 164 us
  local copies, waits for them, and re-layouts: 19.4 us -> 1.42 us
    pallas_call x0 -> x1, Pallas kernels: none -> 56.7 us  [store_results(): pl.pallas_call(store_kernel, out_shape=tuple((jax.ShapeDtypeStruct(r.shap...]
    unnamed x8 -> x0, local copies, waits for them, and re-layouts: 16.8 us -> none
    pallas_call x1, Pallas kernels: 123 us -> 108 us  [local(): pl.pallas_call(functools.partial(block_kernel, n_ts, n_dp, (n_dp * cap) *...]
    broadcast_in_dim x2 -> x0, local copies, waits for them, and re-layouts: 2.61 us -> none  [the longest x1 1.31 us: local(): prenormal_scaling[None]]
where the time goes in v4:
time: 167 us
  Pallas kernels  164 us (98%)
    pallas_call x1, Pallas kernels, local(): pl.pallas_call(functools.partial(block_kernel, n_ts, n_dp, (n_dp * cap) *...  108 us
    pallas_call x1, Pallas kernels, store_results(): pl.pallas_call(store_kernel, out_shape=tuple((jax.ShapeDtypeStruct(r.shap...  56.7 us

profile of v4, /device:TPU:2, one launch (start us, length us, event | category | flops | bytes accessed | tf_op | source)
XLA Modules:
  0.0 167.1 jit_solution(14100950719313240954)
XLA Ops:
  0.6 0.7 stack.9
  1.3 0.7 stack.10
  2.1 0.6 pad_maximum_fusion.vectors_ref
  2.7 107.7 %block_backward.1 = (bf16[64,3584]{1,0:T(8,128)(2,1)}, bf16[448,448]{1,0:T(8,128)(2,1)}, bf16[448,448]{1,0:T(8,128)(2,1)}, bf16[448,448]{1,0:T(8,128)(2,1)}) custom-call(s32[1,256]{1,0:T(1,128)} %kept_row.1, s32[1,256]{1,0:T(1,128)} %kept_row.1, bf16[64,3584]{1,0:T(8,128)(2,1)} %bitcast.8, bf16[64,3584]{1,0:T(8,128)(2,1)} %bitcast.9, ...), custom_call_target="tpu_custom_call" | custom-call | tf_op jit(solution)/shard_map/block_backward/pallas_call | solution.py:625
  110.4 56.7 %store_results.1 = (bf16[1,64,3584]{2,1,0:T(8,128)(2,1)}, bf16[448,448]{1,0:T(8,128)(2,1)}, bf16[448,448]{1,0:T(8,128)(2,1)}, bf16[448,448]{1,0:T(8,128)(2,1)}) custom-call(bf16[1,64,3584]{2,1,0:T(8,128)(2,1)} %bitcast.7, bf16[448,448]{1,0:T(8,128)(2,1)} %get-tuple-element.9.refs_1_, bf16[448,448]{1,0:T(8,128)(2,1)} %get-tuple-element.10.refs_2_, ...), custom_call_target="tpu_custom_call" | custom-call | tf_op jit(solution)/shard_map/store_results/pallas_call | solution.py:598

commit v5 on v4

--- a/solution.py
+++ b/solution.py
@@ -11,17 +11,17 @@
 MESH = pl.DeviceIdType.MESH
 NY = 4
 RS_ORDER = (
-    "acts_start", "terms", ("y", 4), ("y", 3), ("y", 5), ("p", 0), ("p", 1), ("p", 2), ("p", 3), ("s", 4), "acts_relay",
-    ("y", 2), ("y", 6), "x_start", ("s", 3), ("s", 5), ("e", 4), ("z", 0), ("y", 1), ("y", 7), "seen_end", "grow_own",
-    ("s", 2), ("s", 6), ("e", 3), ("e", 5), ("z", 1), ("y", 0), "acts_near", ("s", 1), ("s", 7), ("e", 2), ("e", 6),
-    ("z", 2), ("s", 0), "grow_near", ("e", 1), ("e", 7), ("z", 3), "acts_far", ("e", 0), "x_second", "back_start",
-    "grow_far", "back_end", "x_end",
+    "acts_start", "terms", ("y", 4), ("y", 3), ("y", 5), ("p", 0), ("p", 1), ("p", 2), ("p", 3), ("s", 4),
+    ("y", 2), ("y", 6), "x_start", ("s", 3), ("s", 5), "acts_relay", ("e", 4), ("z", 0), ("y", 1), ("y", 7), ("y", 0),
+    ("s", 2), ("s", 6), ("e", 3), ("e", 5), ("z", 1), ("s", 1), ("s", 7), ("e", 2), ("e", 6), ("z", 2), "seen_end",
+    "grow_own", ("s", 0), ("e", 1), ("e", 7), ("z", 3), ("e", 0), "grow_near", "x_second", "back_start",
+    "grow_far", "back_end", "grow_end", "x_end",
 )
 AG_ORDER = (
     "b1_start", "a1_start", ("f", 0), "b1_relay", ("a", 1), "b1_end", "b2_start", ("a", 2), ("r", 0), ("a", 3),
-    ("r", 1), ("l", 0), ("n", 0), ("r", 2), ("g", 1), ("l", 1), ("n", 1), ("a", 4), ("r", 3), ("l", 2), ("n", 2),
-    ("r", 4), ("g", 2), ("l", 3), ("n", 3), ("r", 5), ("l", 4), ("n", 4), ("r", 6), ("l", 5), ("n", 5),
-    ("r", 7), ("l", 6), ("n", 6), ("g", 3), ("l", 7), ("n", 7), ("g", 4),
+    ("r", 1), ("l", 0), ("r", 2), ("g", 1), ("l", 1), ("a", 4), ("r", 3), ("l", 2),
+    ("r", 4), ("g", 2), ("l", 3), ("r", 5), ("l", 4), ("r", 6), ("l", 5),
+    ("r", 7), ("l", 6), ("g", 3), ("l", 7), "pre", ("g", 4),
 )
 Z_STEPS = (0, -1, 1, -2, 2, -3, 3, 4)
 LANES = 128
@@ -51,10 +51,10 @@
     kept_ref, kept_row, act_ref, cot_ref, vectors_ref, switch_hbm, expand_hbm, contract_hbm,
     token_ref, gate_ref, up_ref, down_ref,
     switch, expand, contract, w_sem,
-    own, slots_f, slots, landed, wide, piece_f, zy, yz, scaled, p1_send, p1_recv, g_send, g_recv,
+    picks, own, slots_f, slots, landed, wide, piece_f, zy, yz, scaled, p1_send, p1_recv, g_send, g_recv,
     pre_gate, pre_up, hidden_grad, gate_in, up_in, acts, hidden, term,
     pair, sib, x_first, x_last, y_first, y_last, y_sum, z_in, z_out, spread, rows_out, slots_out, back, back_f, term_f,
-    sib_send, sib_recv, seen, total, n_send, n_recv, a_send, a_recv, x_send, x_recv, y_send, y_recv, z_send, z_recv, b_send, b_recv,
+    sib_send, sib_recv, seen, total, half_out, half_in, n_send, n_recv, a_send, a_recv, x_send, x_recv, y_send, y_recv, z_send, z_recv, b_send, b_recv,
 ):
     bf16, f32 = jnp.bfloat16, jnp.float32
     nz = n_ts // NY
@@ -99,9 +99,8 @@
     def _(step):
         pl.semaphore_signal(barrier, inc=1, device_id={"ts": lax.rem(me + step, n_ts)}, device_id_type=MESH)
 
-    @pl.loop(1, n_dp)
-    def _(step):
-        pl.semaphore_signal(barrier, inc=1, device_id={"dp": lax.rem(dp + step, n_dp)}, device_id_type=MESH)
+    for where in (sibling, ahead, behind, {"dp": chip(2)}):
+        pl.semaphore_signal(barrier, inc=1, device_id=where, device_id_type=MESH)
 
     weight_copies = [
         pltpu.make_async_copy(src, dst, w_sem.at[i])
@@ -127,7 +126,7 @@
     def _(c):
         slots[c] = slots_f[c].astype(bf16)
 
-    pl.semaphore_wait(barrier, n_ts - 1 + n_dp - 1)
+    pl.semaphore_wait(barrier, n_ts - 1 + 4)
 
 
     def p1_copy(step):
@@ -141,6 +140,13 @@
         p1_copy(step).start()
 
     landed[me] = slots[me]
+
+    @pl.loop(0, n_ts)
+    def _(h):
+        pick = 0
+        for k in range(1, piece_rows):
+            pick = jnp.where(kept_ref[0, n_ts * k + me] // block == h, k, pick)
+        picks[h] = pick
 
     @pl.loop(1, n_ts)
     def _(step):
@@ -200,6 +206,7 @@
     def a1_start():
         share(A1 + 0, piece(zy, me), up)
         share(A1 + 1, piece(zy, me), down)
+        show(0, 0)
 
     def fan_out(j):
         dz = Z_STEPS[j]
@@ -212,10 +219,13 @@
         share(A3 + 2 * j, piece(zy, node(dz, -1), 0), right)
         arrive(g_sems, A2 + 2 * j + 1, piece(zy, node(dz, 1)))
         share(A3 + 2 * j + 1, piece(zy, node(dz, 1), 1), left)
+        show(dz, -1)
+        show(dz, 1)
 
     def last(j):
         arrive(g_sems, A3 + 2 * j, piece(zy, node(Z_STEPS[j], -2), 0))
         arrive(g_sems, A3 + 2 * j + 1, piece(zy, node(Z_STEPS[j], 2), 1))
+        show(Z_STEPS[j], 2)
 
     def along(s):
         which = (0, 1) if s == 4 else (None, None)
@@ -227,8 +237,11 @@
         if s < 4:
             fan_out(2 * s - 1)
             fan_out(2 * s)
+            show(-s, 0)
+            show(s, 0)
         else:
             fan_out(7)
+            show(4, 0)
 
     def b2_start():
         for which in range(2):
@@ -247,60 +260,53 @@
                 elif s == 3 and way == which:
                     share(B2 + 12 + way, group(sign * s, which), to)
 
-    window = seen.shape[3]
     pair_width = 2 * width // n_dp
-
-    def window_at(to):
-        return pl.multiple_of(to // 2 * pair_width + lax.rem(to, 2) * (pair_width - window), LANES)
-
-    def seen_copy(j, step):
-        n = pl.ds(lax.rem(z + Z_STEPS[j] + nz, nz) * NY, NY)
-        to = lax.rem(dp + step, n_dp)
-        index = (step - 1) * nz + j
+    far = (1, -1, 2)
+
+    def seen_copy(rel, index):
+        n = node(rel // NY, lax.rem(rel, NY))
+        at = pl.ds(pl.multiple_of(lax.rem(x + far[index] + nx, nx) * pair_width, LANES), pair_width)
         return pltpu.make_async_remote_copy(
-            zy.at[n, :, pl.ds(window_at(to), window)], seen.at[dp, n], n_send.at[index], n_recv.at[index],
-            device_id={"dp": to}, device_id_type=MESH)
-
-    def show(j):
-        @pl.loop(1, n_dp)
-        def _(step):
-            seen_copy(j, step).start()
-
-    def seen_wait(j):
-        n = pl.ds(lax.rem(z + Z_STEPS[j] + nz, nz) * NY, NY)
-
-        @pl.loop(1, n_dp)
-        def _(step):
-            index = (step - 1) * nz + j
-            source = lax.rem(dp - step + n_dp, n_dp)
-            arrive((n_send, n_recv), index, seen.at[source, n])
-            seen_copy(j, step).wait_send()
+            zy.at[n, :, at], seen.at[x, n], n_send.at[index * n_ts + rel], n_recv.at[index * n_ts + rel],
+            device_id={"dp": chip(far[index])}, device_id_type=MESH)
+
+    def show(dz, dy):
+        for index in range(3):
+            seen_copy(dz % nz * NY + dy % NY, index).start()
+
+    def seen_end():
+        @pl.loop(0, n_ts)
+        def _(rel):
+            n = node(rel // NY, lax.rem(rel, NY))
+            for index in range(3):
+                arrive((n_send, n_recv), index * n_ts + rel, seen.at[lax.rem(x - far[index] + nx, nx), n])
+                seen_copy(rel, index).wait_send()
+
+    def columns(buffer, start, size):
+        return buffer[:, :, pl.ds(start, size)].reshape(cap, size)
+
+    def pre():
+        for copy in weight_copies:
+            copy.wait()
+        pre_gate[...] = jnp.zeros_like(pre_gate)
+        pre_up[...] = jnp.zeros_like(pre_up)
+
+        @pl.loop(0, width // K_TILE)
+        def _(k):
+            at = pl.ds(pl.multiple_of(k * K_TILE, K_TILE), K_TILE)
+            normed = columns(zy, pl.multiple_of(k * K_TILE, K_TILE), K_TILE)
+            pre_gate[...] += dot(normed, switch[:, at], COLS_BY_COLS)
+            pre_up[...] += dot(normed, expand[:, at], COLS_BY_COLS)
 
     steps = dict(
-        b1_start=b1_start, b1_relay=b1_relay, b1_end=b1_end, a1_start=a1_start, b2_start=b2_start)
+        pre=pre,        b1_start=b1_start, b1_relay=b1_relay, b1_end=b1_end, a1_start=a1_start, b2_start=b2_start)
     for step in AG_ORDER:
         if isinstance(step, str):
             steps[step]()
         else:
-            (fan_out, relay, last, along, groups, show)["frlagn".index(step[0])](step[1])
-
-    def columns(buffer, start, size):
-        return buffer[:, :, pl.ds(start, size)].reshape(cap, size)
-
-
-    for copy in weight_copies:
-        copy.wait()
-    pre_gate[...] = jnp.zeros_like(pre_gate)
-    pre_up[...] = jnp.zeros_like(pre_up)
+            (fan_out, relay, last, along, groups)["frlag".index(step[0])](step[1])
+
     hidden_grad[...] = jnp.zeros_like(hidden_grad)
-
-    @pl.loop(0, width // K_TILE)
-    def _(k):
-        at = pl.ds(pl.multiple_of(k * K_TILE, K_TILE), K_TILE)
-        normed = columns(zy, pl.multiple_of(k * K_TILE, K_TILE), K_TILE)
-        pre_gate[...] += dot(normed, switch[:, at], COLS_BY_COLS)
-        pre_up[...] += dot(normed, expand[:, at], COLS_BY_COLS)
-
     for p in range(n_dp // 2):
         at = pl.ds(p * pair_width, pair_width)
         if p < n_dp // 2 - 1:
@@ -321,78 +327,65 @@
         up_back = (grad * gelu_out).astype(bf16)
         gate_in[at, :] = gate_value
         up_in[at, :] = up_back
-        acts[dp, at, :hid] = gate_value
-        acts[dp, at, hid:] = up_back
+        acts[x, at, :hid] = gate_value
+        acts[x, at, hid:] = up_back
         router = jnp.sum(hidden_value.astype(f32) * grad, axis=1, keepdims=True)
         term[i, :, :, width:] = jnp.broadcast_to(router, (n, LANES)).astype(bf16).reshape(NY, piece_rows, LANES)
 
 
     a_sems = (a_send, a_recv)
     halves = (pl.ds(0, cap // 2), pl.ds(cap // 2, cap // 2))
-
-    def other(dx):
-        return lax.rem(x + dx + nx, nx) * 2 + 1 - core
-
-    def part(q, which):
-        return acts.at[q, halves[which]]
+    rows = width // n_dp
+
+    def part(dx, which):
+        return acts.at[lax.rem(x + dx + nx, nx), halves[which]]
 
     def pass_on(index, ref, where):
         send(a_sems, index, ref, ref, where)
 
     def acts_start():
-        pass_on(0, part(dp, 0), ahead)
-        pass_on(2, part(dp, 1), behind)
-        pass_on(1, part(dp, 1), ahead)
-        pass_on(3, part(dp, 0), behind)
-        pass_on(6, acts.at[dp], sibling)
+        pass_on(0, part(0, 0), ahead)
+        pass_on(2, part(0, 1), behind)
+        pass_on(1, part(0, 1), ahead)
+        pass_on(3, part(0, 0), behind)
 
     def acts_relay():
-        arrive(a_sems, 0, part(chip(-1), 0))
-        pass_on(4, part(chip(-1), 0), ahead)
-        pass_on(7, part(chip(-1), 0), sibling)
-        arrive(a_sems, 2, part(chip(1), 1))
-        pass_on(5, part(chip(1), 1), behind)
-        pass_on(10, part(chip(1), 1), sibling)
-
-    def acts_near():
-        arrive(a_sems, 1, part(chip(-1), 1))
-        pass_on(8, part(chip(-1), 1), sibling)
-        arrive(a_sems, 3, part(chip(1), 0))
-        pass_on(9, part(chip(1), 0), sibling)
-
-    def acts_far():
-        arrive(a_sems, 4, part(chip(2), 0))
-        pass_on(11, part(chip(2), 0), sibling)
-        arrive(a_sems, 5, part(chip(2), 1))
-        pass_on(12, part(chip(2), 1), sibling)
-
-    def grow(q):
-        total[...] += dot(seen[q].reshape(cap, window), acts[q], ROWS_BY_ROWS)
+        arrive(a_sems, 0, part(-1, 0))
+        pass_on(4, part(-1, 0), ahead)
+        arrive(a_sems, 2, part(1, 1))
+        pass_on(5, part(1, 1), behind)
+
+    def grow(dx):
+        at = lax.rem(x + dx + nx, nx)
+        total[...] += dot(seen[at].reshape(cap, pair_width), acts[at], ROWS_BY_ROWS)
 
     def grow_own():
-        total[...] = dot(columns(zy, window_at(dp), window), acts[dp], ROWS_BY_ROWS)
-        arrive(a_sems, 6, acts.at[other(0)])
-        grow(other(0))
+        start = pl.multiple_of(x * pair_width, LANES)
+        total[...] = dot(columns(zy, start, pair_width), acts[x], ROWS_BY_ROWS)
 
     def grow_near():
-        for dx, index in ((-1, 7), (1, 9)):
-            grow(chip(dx))
-            arrive(a_sems, index, part(other(dx), 0))
-            arrive(a_sems, index + 1, part(other(dx), 1))
-            grow(other(dx))
+        arrive(a_sems, 1, part(-1, 1))
+        grow(-1)
+        arrive(a_sems, 3, part(1, 0))
+        grow(1)
 
     def grow_far():
-        grow(chip(2))
-        arrive(a_sems, 11, part(other(2), 0))
-        arrive(a_sems, 12, part(other(2), 1))
-        grow(other(2))
-        here = pl.ds(pl.multiple_of(core * (window - rows), 8), rows)
-        gate_ref[...] = (factor * total[here, :hid]).astype(bf16)
-        up_ref[...] = (factor * total[here, hid:]).astype(bf16)
+        arrive(a_sems, 4, part(2, 0))
+        arrive(a_sems, 5, part(2, 1))
+        grow(2)
+        theirs = pl.ds(pl.multiple_of((1 - core) * rows, 16), rows)
+        half_out[...] = (factor * total[theirs, :]).astype(bf16)
+        send(a_sems, 6, half_out, half_in, sibling)
+
+    def grow_end():
+        arrive(a_sems, 6, half_in)
+        here = pl.ds(pl.multiple_of(core * rows, 16), rows)
+        value = factor * total[here, :] + half_in[...].astype(f32)
+        gate_ref[...] = value[:, :hid].astype(bf16)
+        up_ref[...] = value[:, hid:].astype(bf16)
 
     sib_sems, x_sems, y_sems = (sib_send, sib_recv), (x_send, x_recv), (y_send, y_recv)
     z_sems = (z_send, z_recv)
-    rows = width // n_dp
     quarter = hid // 4
     order = (2, 1, -1, 0)
 
@@ -512,9 +505,12 @@
             slots_out.at[to], back.at[me], b_send.at[step], b_recv.at[step],
             device_id={"ts": to}, device_id_type=MESH)
 
-    def back_start():
+    def z_end():
         for way in range(2):
             arrive(z_sems, 6 + way, z_in.at[way, 3])
+
+    def back_start():
+        z_end()
         spread[...] = jnp.zeros_like(spread)
         for t in range(wide_row // LANES):
             at = pl.ds(t * LANES, LANES)
@@ -525,10 +521,7 @@
 
         @pl.loop(0, n_ts)
         def _(h):
-            pick = 0
-            for k in range(1, piece_rows):
-                pick = jnp.where(kept_ref[0, n_ts * k + me] // block == h, k, pick)
-            slots_out[h] = rows_out[pick]
+            slots_out[h] = rows_out[picks[h]]
 
         @pl.loop(1, n_ts)
         def _(step):
@@ -543,6 +536,7 @@
             pltpu.make_async_remote_copy(
                 slots_out.at[source], back.at[source], b_send.at[step], b_recv.at[step],
                 device_id={"ts": source}, device_id_type=MESH).wait_recv()
+            back_copy(step).wait_send()
 
         @pl.loop(0, n_ts)
         def _(c):
@@ -560,14 +554,9 @@
         row_grad = own_inv * (gained - unit * mean) + ((1.0 - own_weight) * summed_dot) * scorer
         token_ref[...] = dot(chosen, row_grad.astype(bf16)).astype(bf16)
 
-    def seen_end():
-        for j in range(nz):
-            seen_wait(j)
-
     jobs = dict(
-        acts_start=acts_start, acts_relay=acts_relay, acts_near=acts_near, acts_far=acts_far, grow_own=grow_own,
-        grow_near=grow_near, grow_far=grow_far, x_start=x_start, x_second=x_second, x_end=x_end, terms=terms,
-        back_start=back_start, back_end=back_end, seen_end=seen_end)
+        acts_start=acts_start, acts_relay=acts_relay, grow_own=grow_own, grow_near=grow_near, grow_far=grow_far,
+        grow_end=grow_end, x_start=x_start, x_second=x_second, x_end=x_end, terms=terms, z_end=z_end, back_start=back_start, back_end=back_end, seen_end=seen_end)
     for job in RS_ORDER:
         if isinstance(job, str):
             jobs[job]()
@@ -577,19 +566,22 @@
     @pl.loop(1, n_ts)
     def _(step):
         p1_copy(step).wait_send()
-        back_copy(step).wait_send()
 
     for copy in pending:
         copy.wait_send()
 
 
 def store_kernel(*refs):
-    sems = refs[-1]
-    count = (len(refs) - 1) // 2
-    copies = [pltpu.make_async_copy(refs[i], refs[count + i], sems.at[i]) for i in range(count)]
-    for copy in copies:
+    count = (len(refs) - 2) // 3
+    sems = refs[-2:]
+    inward = [pltpu.make_async_copy(refs[i], refs[2 * count + i], sems[0].at[i]) for i in range(count)]
+    outward = [pltpu.make_async_copy(refs[2 * count + i], refs[count + i], sems[1].at[i]) for i in range(count)]
+    for copy in inward:
         copy.start()
-    for copy in copies:
+    for first, second in zip(inward, outward):
+        first.wait()
+        second.start()
+    for copy in outward:
         copy.wait()
 
 
@@ -600,7 +592,8 @@
         out_shape=tuple(jax.ShapeDtypeStruct(r.shape, r.dtype) for r in results),
         in_specs=[hbm] * len(results),
         out_specs=(hbm,) * len(results),
-        scratch_shapes=[pltpu.SemaphoreType.DMA((len(results),))],
+        scratch_shapes=[pltpu.VMEM(r.shape, r.dtype) for r in results]
+        + [pltpu.SemaphoreType.DMA((len(results),))] * 2,
         name="store_results",
     )(*results)
 
@@ -617,7 +610,6 @@
     rows = width // n_dp
     piece = cap // n_ts
     tiles = width // LANES
-    window = -(-rows // LANES) * LANES
     pad = -(-(tiles + 1) // 16) * 16
     bf16, f32, dma = jnp.bfloat16, jnp.float32, pltpu.SemaphoreType.DMA
     vmem = pl.BlockSpec(memory_space=pltpu.VMEM)
@@ -634,6 +626,7 @@
         out_specs=(vmem,) * 4,
         scratch_shapes=[
             pltpu.VMEM((hid, width), bf16), pltpu.VMEM((hid, width), bf16), pltpu.VMEM((hid, width), bf16), dma((3,)),
+            pltpu.SMEM((n_ts,), jnp.int32),
             pltpu.VMEM((n_ts, width), f32),
             pltpu.VMEM((n_ts, 2 * tiles, LANES), f32),
             pltpu.VMEM((n_ts, 2 * tiles, LANES), bf16),
@@ -645,7 +638,7 @@
             pltpu.VMEM((cap, width), bf16),
             dma((n_ts,)), dma((n_ts,)), dma((58,)), dma((58,)),
             pltpu.VMEM((cap, hid), f32), pltpu.VMEM((cap, hid), f32), pltpu.VMEM((cap, hid), f32),
-            pltpu.VMEM((cap, hid), bf16), pltpu.VMEM((cap, hid), bf16), pltpu.VMEM((n_dp, cap, 2 * hid), bf16),
+            pltpu.VMEM((cap, hid), bf16), pltpu.VMEM((cap, hid), bf16), pltpu.VMEM((n_dp // 2, cap, 2 * hid), bf16),
             pltpu.VMEM((cap, hid), bf16),
             pltpu.VMEM((nz, NY, piece, width + LANES), bf16),
             pltpu.VMEM((4, 2, hid, rows), bf16),
@@ -664,9 +657,11 @@
             pltpu.VMEM((n_ts, pad, LANES), f32),
             pltpu.VMEM((n_ts, width), f32),
             dma((16,)), dma((16,)),
-            pltpu.VMEM((n_dp, n_ts, piece, window), bf16),
-            pltpu.VMEM((window, 2 * hid), f32),
-            dma((n_dp * nz,)), dma((n_dp * nz,)), dma((13,)), dma((13,)),
+            pltpu.VMEM((n_dp // 2, n_ts, piece, 2 * rows), bf16),
+            pltpu.VMEM((2 * rows, 2 * hid), f32),
+            pltpu.VMEM((rows, 2 * hid), bf16),
+            pltpu.VMEM((rows, 2 * hid), bf16),
+            dma((3 * n_ts,)), dma((3 * n_ts,)), dma((7,)), dma((7,)),
             dma((12,)), dma((12,)), dma((6 * nz,)), dma((6 * nz,)),
             dma((8,)), dma((8,)), dma((n_ts,)), dma((n_ts,)),
         ],

time: 167 us -> 110 us (0.66)
  Pallas kernels: 164 us -> 107 us
    pallas_call x1, Pallas kernels: 56.7 us -> 2.31 us  [store_results(): pl.pallas_call(store_kernel, out_shape=tuple((jax.ShapeDtypeStruct(r.shap...]
    pallas_call x1, Pallas kernels: 108 us -> 105 us  [local(): pl.pallas_call(functools.partial(block_kernel, n_ts, n_dp, (n_dp * cap) *...]
where the time goes in v5:
time: 110 us
  Pallas kernels  107 us (97%)
  local copies, waits for them, and re-layouts  1.42 us (1%)
    pallas_call x1, Pallas kernels, local(): pl.pallas_call(functools.partial(block_kernel, n_ts, n_dp, (n_dp * cap) *...  105 us
    pallas_call x1, Pallas kernels, store_results(): pl.pallas_call(store_kernel, out_shape=tuple((jax.ShapeDtypeStruct(r.shap...  2.31 us

profile of v5, /device:TPU:2, one launch (start us, length us, event | category | flops | bytes accessed | tf_op | source)
XLA Modules:
  0.0 110.1 jit_solution(13569468343104192003)
XLA Ops:
  0.6 0.7 stack.9
  1.3 0.7 stack.10
  2.1 0.6 pad_maximum_fusion.vectors_ref
  2.7 105.1 %block_backward.1 = (bf16[64,3584]{1,0:T(8,128)(2,1)}, bf16[448,448]{1,0:T(8,128)(2,1)}, bf16[448,448]{1,0:T(8,128)(2,1)}, bf16[448,448]{1,0:T(8,128)(2,1)}) custom-call(s32[1,256]{1,0:T(1,128)} %kept_row.1, s32[1,256]{1,0:T(1,128)} %kept_row.1, bf16[64,3584]{1,0:T(8,128)(2,1)} %bitcast.8, bf16[64,3584]{1,0:T(8,128)(2,1)} %bitcast.9, ...), custom_call_target="tpu_custom_call" | custom-call | tf_op jit(solution)/shard_map/block_backward/pallas_call | solution.py:617
  107.8 2.3 %store_results.1 = (bf16[1,64,3584]{2,1,0:T(8,128)(2,1)}, bf16[448,448]{1,0:T(8,128)(2,1)}, bf16[448,448]{1,0:T(8,128)(2,1)}, bf16[448,448]{1,0:T(8,128)(2,1)}) custom-call(bf16[1,64,3584]{2,1,0:T(8,128)(2,1)} %bitcast.7, bf16[448,448]{1,0:T(8,128)(2,1)} %get-tuple-element.9.refs_1_, bf16[448,448]{1,0:T(8,128)(2,1)} %get-tuple-element.10.refs_2_, ...), custom_call_target="tpu_custom_call" | custom-call | tf_op jit(solution)/shard_map/store_results/pallas_call | solution.py:590

commit v6 on v5

--- a/solution.py
+++ b/solution.py
@@ -12,16 +12,18 @@
 NY = 4
 RS_ORDER = (
     "acts_start", "terms", ("y", 4), ("y", 3), ("y", 5), ("p", 0), ("p", 1), ("p", 2), ("p", 3), ("s", 4),
-    ("y", 2), ("y", 6), "x_start", ("s", 3), ("s", 5), "acts_relay", ("e", 4), ("z", 0), ("y", 1), ("y", 7), ("y", 0),
-    ("s", 2), ("s", 6), ("e", 3), ("e", 5), ("z", 1), ("s", 1), ("s", 7), ("e", 2), ("e", 6), ("z", 2), "seen_end",
-    "grow_own", ("s", 0), ("e", 1), ("e", 7), ("z", 3), ("e", 0), "grow_near", "x_second", "back_start",
+    ("y", 2), ("y", 6), "x_start", ("s", 3), ("s", 5), "acts_relay", ("y", 1), ("y", 7), ("y", 0),
+    ("s", 2), ("s", 6), ("e", 4), ("e", 3), ("e", 5), "z_first", ("s", 1), ("s", 7), ("e", 2), ("e", 6), "z_second",
+    ("s", 0), "seen_end", "grow_own", ("e", 1), ("e", 7), "z_third", ("e", 0), "grow_near", "x_second", "back_start",
     "grow_far", "back_end", "grow_end", "x_end",
 )
+B_STEPS = (0, -1, 1, 2)
 AG_ORDER = (
-    "b1_start", "a1_start", ("f", 0), "b1_relay", ("a", 1), "b1_end", "b2_start", ("a", 2), ("r", 0), ("a", 3),
-    ("r", 1), ("l", 0), ("r", 2), ("g", 1), ("l", 1), ("a", 4), ("r", 3), ("l", 2),
-    ("r", 4), ("g", 2), ("l", 3), ("r", 5), ("l", 4), ("r", 6), ("l", 5),
-    ("r", 7), ("l", 6), ("g", 3), ("l", 7), "pre", ("g", 4),
+    "b1_start", "a1_start", ("f", 0), ("c", 0, 0), "b1_relay", ("c", 1, 0), ("c", 2, 0), ("a", 1), ("c", 0, 1), ("r", 0),
+    "b1_end", ("c", 3, 0), ("a", 2), ("c", 1, 1), ("c", 2, 1), ("c", 0, 2), ("r", 1), ("l", 0), ("r", 2), ("c", 3, 1),
+    ("a", 3), ("c", 1, 2), ("c", 2, 2), ("l", 1), ("c", 0, 3), ("r", 3), ("l", 2), ("a", 4), ("r", 4), ("c", 3, 2),
+    ("c", 1, 3), ("c", 2, 3), ("l", 3), ("r", 5), ("l", 4), ("c", 0, 4), ("r", 6), ("l", 5), ("c", 3, 3), ("r", 7),
+    ("c", 1, 4), ("c", 2, 4), ("l", 6), ("l", 7), "pre", ("c", 3, 4),
 )
 Z_STEPS = (0, -1, 1, -2, 2, -3, 3, 4)
 LANES = 128
@@ -181,13 +183,10 @@
     def piece(buffer, n, which=None):
         return buffer.at[n] if which is None else buffer.at[n, :, cut(buffer, which)]
 
-    def group(dz, which):
-        return yz.at[pl.ds(lax.rem(z + dz + nz, nz) * NY + which * (NY // 2), NY // 2)]
-
     def share(index, ref, where):
         send(g_sems, index, ref, ref, where)
 
-    B1, A1, B2, A2, A3 = 0, 4, 12, 26, 42
+    B1, A1, A2, A3, B2 = 0, 4, 12, 28, 44
 
     def b1_start():
         share(B1 + 0, piece(yz, me), right)
@@ -243,22 +242,16 @@
             fan_out(7)
             show(4, 0)
 
-    def b2_start():
-        for which in range(2):
-            share(B2 + 2 * which, group(0, which), up)
-            share(B2 + 2 * which + 1, group(0, which), down)
-
-    def groups(s):
-        for which in range(2):
-            for way, to, sign in ((0, up, -1), (1, down, 1)):
-                if s == 4 and way != which:
-                    continue
-                index = B2 + 12 + way if s == 4 else B2 + 4 * (s - 1) + 2 * which + way
-                arrive(g_sems, index, group(sign * s, which))
-                if s < 3:
-                    share(B2 + 4 * s + 2 * which + way, group(sign * s, which), to)
-                elif s == 3 and way == which:
-                    share(B2 + 12 + way, group(sign * s, which), to)
+    def chain(k, s):
+        dy, one_way = B_STEPS[k], k // 2
+        for way, to, sign in ((0, up, -1), (1, down, 1)):
+            if s == 4 and way != one_way:
+                continue
+            ref = piece(yz, node(sign * s, dy))
+            if s > 0:
+                arrive(g_sems, B2 + 8 * k + 2 * (s - 1) + way, ref)
+            if s < 3 or (s == 3 and way == one_way):
+                share(B2 + 8 * k + 2 * s + way, ref, to)
 
     pair_width = 2 * width // n_dp
     far = (1, -1, 2)
@@ -299,12 +292,12 @@
             pre_up[...] += dot(normed, expand[:, at], COLS_BY_COLS)
 
     steps = dict(
-        pre=pre,        b1_start=b1_start, b1_relay=b1_relay, b1_end=b1_end, a1_start=a1_start, b2_start=b2_start)
+        pre=pre,        b1_start=b1_start, b1_relay=b1_relay, b1_end=b1_end, a1_start=a1_start)
     for step in AG_ORDER:
         if isinstance(step, str):
             steps[step]()
         else:
-            (fan_out, relay, last, along, groups)["frlag".index(step[0])](step[1])
+            (fan_out, relay, last, along, chain)["frlac".index(step[0])](*step[1:])
 
     hidden_grad[...] = jnp.zeros_like(hidden_grad)
     for p in range(n_dp // 2):
@@ -483,21 +476,26 @@
         value = term[at_z(i), y].astype(f32) + y_last[0, i].astype(f32)
         y_sum[i] = (value + y_last[1, i].astype(f32)).astype(bf16)
 
-    def z_step(s):
-        for way, to in ((0, up), (1, down)):
-            mine = 4 - s if way == 0 else 4 + s
-            if s == 0:
-                send(z_sems, way, y_sum.at[4, :, cols[way]], z_in.at[way, 0, :, cols[way]], to)
-                continue
-            if s == 1:
-                arrive(z_sems, way, z_in.at[way, 0, :, cols[way]])
-                z_out[way, s] = y_sum[mine]
-                both = y_sum[mine, :, cols[way]].astype(f32) + z_in[way, 0, :, cols[way]].astype(f32)
-                z_out[way, s, :, cols[way]] = both.astype(bf16)
-            else:
-                arrive(z_sems, 2 * (s - 1) + way, z_in.at[way, s - 1])
-                z_out[way, s] = (y_sum[mine].astype(f32) + z_in[way, s - 1].astype(f32)).astype(bf16)
-            send(z_sems, 2 * s + way, z_out.at[way, s], z_in.at[way, s], to)
+    def z_first():
+        for way, sign in ((0, 1), (1, -1)):
+            send(z_sems, 4 * way, y_sum.at[4, :, cols[way]], z_in.at[way, 0, :, cols[way]], {"ts": node(2 * sign, 0)})
+            send(z_sems, 4 * way + 1, y_sum.at[3 if way == 0 else 5], z_in.at[way, 1], {"ts": node(sign, 0)})
+
+    def z_second():
+        for way, sign in ((0, 1), (1, -1)):
+            arrive(z_sems, 4 * way + 1, z_in.at[way, 1])
+            arrive(z_sems, 4 * way, z_in.at[way, 0, :, cols[way]])
+            mine = 2 if way == 0 else 6
+            rest = cols[1 - way]
+            z_out[way, :, rest] = (
+                y_sum[mine, :, rest].astype(f32) + z_in[way, 1, :, rest].astype(f32)).astype(bf16)
+            value = y_sum[mine, :, cols[way]].astype(f32) + z_in[way, 1, :, cols[way]].astype(f32)
+            z_out[way, :, cols[way]] = (value + z_in[way, 0, :, cols[way]].astype(f32)).astype(bf16)
+            send(z_sems, 4 * way + 2, z_out.at[way], z_in.at[way, 2], {"ts": node(2 * sign, 0)})
+
+    def z_third():
+        for way, sign in ((0, 1), (1, -1)):
+            send(z_sems, 4 * way + 3, y_sum.at[1 if way == 0 else 7], z_in.at[way, 3], {"ts": node(sign, 0)})
 
     def back_copy(step):
         to = lax.rem(me + step, n_ts)
@@ -507,15 +505,18 @@
 
     def z_end():
         for way in range(2):
-            arrive(z_sems, 6 + way, z_in.at[way, 3])
+            arrive(z_sems, 4 * way + 2, z_in.at[way, 2])
+            arrive(z_sems, 4 * way + 3, z_in.at[way, 3])
 
     def back_start():
         z_end()
         spread[...] = jnp.zeros_like(spread)
         for t in range(wide_row // LANES):
             at = pl.ds(t * LANES, LANES)
-            value = y_sum[0, :, at].astype(f32) + z_in[0, 3, :, at].astype(f32)
-            spread[:, t, :] = value + z_in[1, 3, :, at].astype(f32)
+            value = y_sum[0, :, at].astype(f32)
+            for way in range(2):
+                value += z_in[way, 2, :, at].astype(f32) + z_in[way, 3, :, at].astype(f32)
+            spread[:, t, :] = value
         for k in range(piece_rows):
             rows_out[k] = spread[k].astype(bf16)
 
@@ -556,12 +557,12 @@
 
     jobs = dict(
         acts_start=acts_start, acts_relay=acts_relay, grow_own=grow_own, grow_near=grow_near, grow_far=grow_far,
-        grow_end=grow_end, x_start=x_start, x_second=x_second, x_end=x_end, terms=terms, z_end=z_end, back_start=back_start, back_end=back_end, seen_end=seen_end)
+        grow_end=grow_end, x_start=x_start, x_second=x_second, x_end=x_end, terms=terms, z_first=z_first, z_second=z_second, z_third=z_third, z_end=z_end, back_start=back_start, back_end=back_end, seen_end=seen_end)
     for job in RS_ORDER:
         if isinstance(job, str):
             jobs[job]()
         else:
-            (partials, y_start, y_second, y_end, z_step)["pysez".index(job[0])](job[1])
+            (partials, y_start, y_second, y_end)["pyse".index(job[0])](job[1])
 
     @pl.loop(1, n_ts)
     def _(step):
@@ -636,7 +637,7 @@
             pltpu.VMEM((n_ts, piece, width + 2 * rows), bf16),
             pltpu.VMEM((n_ts, piece, width - 2 * rows), bf16),
             pltpu.VMEM((cap, width), bf16),
-            dma((n_ts,)), dma((n_ts,)), dma((58,)), dma((58,)),
+            dma((n_ts,)), dma((n_ts,)), dma((76,)), dma((76,)),
             pltpu.VMEM((cap, hid), f32), pltpu.VMEM((cap, hid), f32), pltpu.VMEM((cap, hid), f32),
             pltpu.VMEM((cap, hid), bf16), pltpu.VMEM((cap, hid), bf16), pltpu.VMEM((n_dp // 2, cap, 2 * hid), bf16),
             pltpu.VMEM((cap, hid), bf16),
@@ -649,7 +650,7 @@
             pltpu.VMEM((2, nz, piece, width + LANES), bf16),
             pltpu.VMEM((nz, piece, width + LANES), bf16),
             pltpu.VMEM((2, 4, piece, width + LANES), bf16),
-            pltpu.VMEM((2, 4, piece, width + LANES), bf16),
+            pltpu.VMEM((2, piece, width + LANES), bf16),
             pltpu.VMEM((piece, pad, LANES), f32),
             pltpu.VMEM((piece, pad, LANES), bf16),
             pltpu.VMEM((n_ts, pad, LANES), bf16),

time: 110 us -> 107 us (0.973)
  Pallas kernels: 107 us -> 104 us
    pallas_call x1, Pallas kernels: 105 us -> 101 us  [local(): pl.pallas_call(functools.partial(block_kernel, n_ts, n_dp, (n_dp * cap) *...]
where the time goes in v6:
time: 107 us; the launch traced here: 106 us
  Pallas kernels  104 us (97%)
  local copies, waits for them, and re-layouts  1.42 us (1%)
    pallas_call x1, Pallas kernels, local(): pl.pallas_call(functools.partial(block_kernel, n_ts, n_dp, (n_dp * cap) *...  101 us
    pallas_call x1, Pallas kernels, store_results(): pl.pallas_call(store_kernel, out_shape=tuple((jax.ShapeDtypeStruct(r.shap...  2.31 us

profile of v6, /device:TPU:2, one launch (start us, length us, event | category | flops | bytes accessed | tf_op | source)
XLA Modules:
  0.0 106.2 jit_solution(14207102653840927926)
XLA Ops:
  0.6 0.7 stack.9
  1.3 0.7 stack.10
  2.1 0.6 pad_maximum_fusion.vectors_ref
  2.7 101.2 %block_backward.1 = (bf16[64,3584]{1,0:T(8,128)(2,1)}, bf16[448,448]{1,0:T(8,128)(2,1)}, bf16[448,448]{1,0:T(8,128)(2,1)}, bf16[448,448]{1,0:T(8,128)(2,1)}) custom-call(s32[1,256]{1,0:T(1,128)} %kept_row.1, s32[1,256]{1,0:T(1,128)} %kept_row.1, bf16[64,3584]{1,0:T(8,128)(2,1)} %bitcast.8, bf16[64,3584]{1,0:T(8,128)(2,1)} %bitcast.9, ...), custom_call_target="tpu_custom_call" | custom-call | tf_op jit(solution)/shard_map/block_backward/pallas_call | solution.py:618
  103.9 2.3 %store_results.1 = (bf16[1,64,3584]{2,1,0:T(8,128)(2,1)}, bf16[448,448]{1,0:T(8,128)(2,1)}, bf16[448,448]{1,0:T(8,128)(2,1)}, bf16[448,448]{1,0:T(8,128)(2,1)}) custom-call(bf16[1,64,3584]{2,1,0:T(8,128)(2,1)} %bitcast.7, bf16[448,448]{1,0:T(8,128)(2,1)} %get-tuple-element.9.refs_1_, bf16[448,448]{1,0:T(8,128)(2,1)} %get-tuple-element.10.refs_2_, ...), custom_call_target="tpu_custom_call" | custom-call | tf_op jit(solution)/shard_map/store_results/pallas_call | solution.py:591

commit v7 on v6

--- a/solution.py
+++ b/solution.py
@@ -50,7 +50,7 @@
 
 def block_kernel(
     n_ts, n_dp, factor,
-    kept_ref, kept_row, act_ref, cot_ref, vectors_ref, switch_hbm, expand_hbm, contract_hbm,
+    kept_ref, kept_row, act_ref, cot_ref, gain_ref, scorer_ref, switch_hbm, expand_hbm, contract_hbm,
     token_ref, gate_ref, up_ref, down_ref,
     switch, expand, contract, w_sem,
     picks, own, slots_f, slots, landed, wide, piece_f, zy, yz, scaled, p1_send, p1_recv, g_send, g_recv,
@@ -143,6 +143,13 @@
 
     landed[me] = slots[me]
 
+    gain = gain_ref[...].astype(f32).reshape(1, width)
+    scorer = scorer_ref[...].astype(f32).reshape(1, width)
+    own_f = own[...]
+    own_inv = lax.rsqrt(jnp.sum(own_f * own_f, axis=1, keepdims=True) * (1.0 / width) + epsilon)
+    own_weight = jax.nn.sigmoid(jnp.sum(own_f * scorer, axis=1, keepdims=True))
+    own[...] = own_f * own_inv
+
     @pl.loop(0, n_ts)
     def _(h):
         pick = 0
@@ -163,8 +170,6 @@
     for t in range(2 * tiles):
         piece_f[:, t * LANES:(t + 1) * LANES] = wide[:, t, :]
 
-    gain = vectors_ref[0:1, :].astype(f32)
-    scorer = vectors_ref[1:2, :].astype(f32)
     row_f = piece_f[:, :width]
     inv_rms = lax.rsqrt(jnp.sum(row_f * row_f, axis=1, keepdims=True) * (1.0 / width) + epsilon)
     weight = jax.nn.sigmoid(jnp.sum(row_f * scorer, axis=1, keepdims=True))
@@ -546,10 +551,7 @@
         for t in range(tiles):
             term_f[:, t * LANES:(t + 1) * LANES] = back_f[:, t, :]
         summed_dot = back_f[:, tiles, :][:, :1]
-        own_f = own[...]
-        own_inv = lax.rsqrt(jnp.sum(own_f * own_f, axis=1, keepdims=True) * (1.0 / width) + epsilon)
-        own_weight = jax.nn.sigmoid(jnp.sum(own_f * scorer, axis=1, keepdims=True))
-        unit = own_f * own_inv
+        unit = own[...]
         gained = term_f[...] * gain
         mean = jnp.sum(gained * unit, axis=1, keepdims=True) * (1.0 / width)
         row_grad = own_inv * (gained - unit * mean) + ((1.0 - own_weight) * summed_dot) * scorer
@@ -623,7 +625,7 @@
             jax.ShapeDtypeStruct((rows, hid), bf16),
             jax.ShapeDtypeStruct((hid, rows), bf16),
         ),
-        in_specs=[pl.BlockSpec(memory_space=pltpu.SMEM)] + [vmem] * 4 + [hbm] * 3,
+        in_specs=[pl.BlockSpec(memory_space=pltpu.SMEM)] + [vmem] * 5 + [hbm] * 3,
         out_specs=(vmem,) * 4,
         scratch_shapes=[
             pltpu.VMEM((hid, width), bf16), pltpu.VMEM((hid, width), bf16), pltpu.VMEM((hid, width), bf16), dma((3,)),
@@ -671,7 +673,7 @@
         name="block_backward",
     )(
         kept_locations, kept_locations, block_activity[0], result_cotangent[0],
-        jnp.stack([prenormal_scaling, scorer_matrix]), switch_matrix.T, expand_matrix.T, contract_matrix,
+        prenormal_scaling, scorer_matrix, switch_matrix.T, expand_matrix.T, contract_matrix,
     )
     return store_results(token[None], gate, up, down)
 

time: 107 us -> 105 us (0.981)
  local copies, waits for them, and re-layouts: 1.42 us -> 0 us
    another operation x2 -> x0, local copies, waits for them, and re-layouts: 1.42 us -> none  [local(): jnp.stack([prenormal_scaling, scorer_matrix])]
where the time goes in v7:
time: 105 us; the launch traced here: 104 us
  Pallas kernels  104 us (99%)
    pallas_call x1, Pallas kernels, local(): pl.pallas_call(functools.partial(block_kernel, n_ts, n_dp, (n_dp * cap) *...  101 us
    pallas_call x1, Pallas kernels, store_results(): pl.pallas_call(store_kernel, out_shape=tuple((jax.ShapeDtypeStruct(r.shap...  2.31 us

profile of v7, /device:TPU:2, one launch (start us, length us, event | category | flops | bytes accessed | tf_op | source)
XLA Modules:
  0.0 104.3 jit_solution(14153529636534937645)
XLA Ops:
  0.6 101.4 %block_backward.1 = (bf16[64,3584]{1,0:T(8,128)(2,1)}, bf16[448,448]{1,0:T(8,128)(2,1)}, bf16[448,448]{1,0:T(8,128)(2,1)}, bf16[448,448]{1,0:T(8,128)(2,1)}) custom-call(s32[1,256]{1,0:T(1,128)} %kept_row.1, s32[1,256]{1,0:T(1,128)} %kept_row.1, bf16[64,3584]{1,0:T(8,128)(2,1)} %bitcast.8, bf16[64,3584]{1,0:T(8,128)(2,1)} %bitcast.9, ...), custom_call_target="tpu_custom_call" | custom-call | tf_op jit(solution)/shard_map/block_backward/pallas_call | solution.py:620
  102.0 2.3 %store_results.1 = (bf16[1,64,3584]{2,1,0:T(8,128)(2,1)}, bf16[448,448]{1,0:T(8,128)(2,1)}, bf16[448,448]{1,0:T(8,128)(2,1)}, bf16[448,448]{1,0:T(8,128)(2,1)}) custom-call(bf16[1,64,3584]{2,1,0:T(8,128)(2,1)} %bitcast.7, bf16[448,448]{1,0:T(8,128)(2,1)} %get-tuple-element.9.refs_1_, bf16[448,448]{1,0:T(8,128)(2,1)} %get-tuple-element.10.refs_2_, ...), custom_call_target="tpu_custom_call" | custom-call | tf_op jit(solution)/shard_map/store_results/pallas_call | solution.py:593

commit v8 on v7

--- a/solution.py
+++ b/solution.py
@@ -139,7 +139,7 @@
 
     @pl.loop(1, n_ts)
     def _(step):
-        p1_copy(step).start()
+        p1_copy(lax.rem(step + n_ts // 2 - 2, n_ts - 1) + 1).start()
 
     landed[me] = slots[me]
 
@@ -531,7 +531,7 @@
 
         @pl.loop(1, n_ts)
         def _(step):
-            back_copy(step).start()
+            back_copy(lax.rem(step + n_ts // 2 - 2, n_ts - 1) + 1).start()
 
         back[me] = slots_out[me]
 

time: 105 us -> 104 us (level); the launches traced: 104 us -> 104 us
  no operation moved by 1% of the time
where the time goes in v8:
time: 104 us
  Pallas kernels  104 us (100%)
    pallas_call x1, Pallas kernels, local(): pl.pallas_call(functools.partial(block_kernel, n_ts, n_dp, (n_dp * cap) *...  101 us
    pallas_call x1, Pallas kernels, store_results(): pl.pallas_call(store_kernel, out_shape=tuple((jax.ShapeDtypeStruct(r.shap...  2.31 us

profile of v8, /device:TPU:2, one launch (start us, length us, event | category | flops | bytes accessed | tf_op | source)
XLA Modules:
  0.0 104.4 jit_solution(9891251909859021523)
XLA Ops:
  0.6 101.4 %block_backward.1 = (bf16[64,3584]{1,0:T(8,128)(2,1)}, bf16[448,448]{1,0:T(8,128)(2,1)}, bf16[448,448]{1,0:T(8,128)(2,1)}, bf16[448,448]{1,0:T(8,128)(2,1)}) custom-call(s32[1,256]{1,0:T(1,128)} %kept_row.1, s32[1,256]{1,0:T(1,128)} %kept_row.1, bf16[64,3584]{1,0:T(8,128)(2,1)} %bitcast.8, bf16[64,3584]{1,0:T(8,128)(2,1)} %bitcast.9, ...), custom_call_target="tpu_custom_call" | custom-call | tf_op jit(solution)/shard_map/block_backward/pallas_call | solution.py:620
  102.1 2.3 %store_results.1 = (bf16[1,64,3584]{2,1,0:T(8,128)(2,1)}, bf16[448,448]{1,0:T(8,128)(2,1)}, bf16[448,448]{1,0:T(8,128)(2,1)}, bf16[448,448]{1,0:T(8,128)(2,1)}) custom-call(bf16[1,64,3584]{2,1,0:T(8,128)(2,1)} %bitcast.7, bf16[448,448]{1,0:T(8,128)(2,1)} %get-tuple-element.9.refs_1_, bf16[448,448]{1,0:T(8,128)(2,1)} %get-tuple-element.10.refs_2_, ...), custom_call_target="tpu_custom_call" | custom-call | tf_op jit(solution)/shard_map/store_results/pallas_call | solution.py:593
